TPU v7x, 768 devices: a whole 4x8x12 slice. The times are simulated.
768 devices in a mesh: rep: 48 (over z, x_hi, core), shard: 16 (over x_lo, y).
Axes of the slice: x: 4 (x_hi: 2, x_lo: 2; x = x_hi * 2 + x_lo), y: 8, z: 12, core: 2. Of those that a mesh axis runs over, the one named last changes fastest.
Arguments:
- seq_lengths: int32 [768, 2], P(('rep', 'shard')), may hold values from 1 to 64, as said below
- token_ids: int32 [98304], P(('rep', 'shard')), may hold values from 4 to 28
- masked: int32 [98304], P(('rep', 'shard')), may hold values 0 or 1
- embed_table: bfloat16 [33, 5120], replicated
- ln_gain: float32 [5120], replicated, may hold values from 0.25 to 4
- grad_resid: bfloat16 [98304, 5120], P(('rep', 'shard')), may hold values from -0.1875 to 0.1875
- grad_normed: bfloat16 [98304, 5120], P(('rep', 'shard')), may hold values from -0.1875 to 0.1875
Outputs:
- layer_grads: float32 [15360], P('shard')
- embed_grads: float32 [168960], P('shard')
Inputs may be any that keep to these rules, and one draw needn't show every extreme that they name: `seq_lengths`: on every device one of its sequences has length exactly 64; the others have lengths of 1 to 64.
All inputs are finite; a program needn't handle non-finite values. No bound on the sum of `masked` on one device may be relied on, other than what follows from the above.
Results may differ from a plain program's by a relative error of at most 0.0003.
Values sent between devices are 32-bit elements; how exact they have to be, the bound alone decides.
No kernel may reach another device: no remote copies, remote signals or barrier semaphores. Data moves between devices by JAX's collectives and lax.ppermute only.
A program may use at most 32 MiB of HBM per device.

v0:
```python
import jax
import jax.numpy as jnp
from jax import lax
from jax.sharding import PartitionSpec as P


def token_weights(lengths, masked):
    slot_count = masked.shape[0]
    seq_ends = jnp.cumsum(lengths)
    seq_starts = seq_ends - lengths
    position = jnp.arange(slot_count, dtype=jnp.int32)[:, None]
    member = ((position >= seq_starts[None, :]) & (position < seq_ends[None, :])).astype(
        jnp.float32
    )
    masked_f = masked.astype(jnp.float32)
    masked_count = jnp.sum(member * masked_f[:, None], axis=0)
    mask_ratio = masked_count / lengths.astype(jnp.float32)
    factor = 0.88 / jnp.maximum(1.0 - mask_ratio, 0.5)
    live_rows = jnp.sum(member, axis=1)
    token_scale = jnp.sum(member * factor[None, :], axis=1)
    return (live_rows, live_rows * (1.0 - masked_f) * token_scale)


def reduce_bucket(flat_sum):
    owned = lax.psum_scatter(flat_sum, "shard", scatter_dimension=0, tiled=True)
    return lax.psum(owned, "rep")


def embedding_sums(onehot, weight, resid_cot, normed_cot, normed, inv_std, ln_gain):
    scaled = normed_cot * ln_gain[None, :]
    through = inv_std * (
        scaled
        - jnp.mean(scaled, axis=1, keepdims=True)
        - normed * jnp.mean(scaled * normed, axis=1, keepdims=True)
    )
    flowing = (resid_cot + through) * weight[:, None]
    return jnp.dot(onehot.astype(jnp.float32).T, flowing, precision=lax.Precision.HIGHEST)


def on_device(seq_lengths, token_ids, masked, embed_table, ln_gain, grad_resid, grad_normed):
    live_rows, weight = token_weights(seq_lengths[0], masked)
    vocab_size = embed_table.shape[0]
    onehot = (token_ids[:, None] == jnp.arange(vocab_size, dtype=jnp.int32)[None, :]).astype(
        jnp.bfloat16
    )
    looked_up = jnp.dot(onehot, embed_table, preferred_element_type=jnp.float32)
    embedded = looked_up * weight[:, None]
    row_mean = jnp.mean(embedded, axis=1, keepdims=True)
    centered = embedded - row_mean
    inv_std = lax.rsqrt(jnp.mean(centered * centered, axis=1, keepdims=True) + 1e-05)
    normed = centered * inv_std
    resid_cot = grad_resid.astype(jnp.float32) * live_rows[:, None]
    normed_cot = grad_normed.astype(jnp.float32) * live_rows[:, None]
    layer_sums = jnp.stack(
        [
            jnp.sum(resid_cot, axis=0),
            jnp.sum(normed_cot * normed, axis=0),
            jnp.sum(normed_cot, axis=0),
        ]
    )
    layer_owned = reduce_bucket(layer_sums.reshape(-1))
    embed_sums = embedding_sums(onehot, weight, resid_cot, normed_cot, normed, inv_std, ln_gain)
    return (layer_owned, reduce_bucket(embed_sums.reshape(-1)))


def solution(mesh):
    in_specs = (
        P(("rep", "shard"), None),
        P(("rep", "shard")),
        P(("rep", "shard")),
        P(),
        P(),
        P(("rep", "shard"), None),
        P(("rep", "shard"), None),
    )
    out_specs = (P("shard"), P("shard"))
    return jax.shard_map(
        on_device, mesh=mesh, in_specs=in_specs, out_specs=out_specs, check_vma=False
    )
```

profile of v0, /device:TPU:1, one launch (start us, length us, event | category | flops | bytes accessed | tf_op | source)
XLA Modules:
  0.0 368.0 jit_solution(5658298702690533281)
XLA Ops:
  7.2 0.0 copy-start
  7.2 0.0 all-reduce.5.cloned.1.call-start
  7.2 0.7 convert_element_type.21
  7.9 0.8 reduce-window.4
  8.8 0.7 fusion.21
  9.4 0.2 select_reduce_fusion.1
  9.6 0.7 divide_bitcast_fusion
  10.3 0.1 select_reduce_fusion
  10.3 0.7 multiply_multiply_fusion
  11.0 0.0 copy-done
  11.0 0.0 copy-start.1
  11.0 0.0 copy-start.2
  11.0 0.0 copy-start.3
  11.0 1.4 fusion.22
  12.5 0.4 multiply_reduce_fusion.2
  12.9 0.0 copy-done.1
  12.9 0.0 copy-done.2
  12.9 0.0 copy-done.3
  12.9 0.0 copy-start.4
  13.0 1.5 multiply_reduce_fusion
  14.5 0.0 copy-done.4
  14.5 2.3 fusion
  16.8 1.0 reshape.49
  17.8 0.0 all-reduce.5.cloned.1.call-update
  17.8 0.1 pad_maximum_fusion
  17.9 1.3 dynamic-slice
  20.5 52.2 %all-reduce = f32[15360]{0:T(1024)S(1)} all-reduce(f32[15360]{0:T(1024)S(1)} %reshape.48), channel_id=2, replica_groups=mesh['rep'=48,'shard'=16] {'shard'}, use_global_device_ids=true, to_apply=%region_9.10.clone | all-reduce | flops 15360 | bytes 122880
  72.7 0.1 dynamic-slice.1
  72.7 89.1 %all-reduce.5.cloned.1.call-done = f32[168960]{0:T(1024)} async-done(((f32[168960]{0:T(1024)}), f32[168960]{0:T(1024)}) %all-reduce.5.cloned.1.call-update) | async-done | bytes 675856
  161.9 0.9 dynamic-slice.3
  162.7 198.4 %all-reduce.2 = (f32[960]{0:T(1024)}, f32[10560]{0:T(1024)}) all-reduce(f32[960]{0:T(1024)S(1)} %dynamic-slice.1, f32[10560]{0:T(1024)S(1)} %dynamic-slice.3), channel_id=1, replica_groups=mesh['rep'=48,'shard'=16] {'rep'}, use_global_device_ids=true, to_apply=%region_10.11 | all-reduce | flops 11520 | bytes 92160 | tf_op jit(solution)/shard_map/psum | solution.py:26
  (4 shorter events, 0.1 us)
Async XLA Ops:
  7.2 3.9 %copy-start = (bf16[33,5120]{1,0:T(8,128)(2,1)S(1)}, bf16[33,5120]{1,0:T(8,128)(2,1)}, u32[]{:S(2)}) copy-start(bf16[33,5120]{1,0:T(8,128)(2,1)} %param.10) | copy-start | bytes 1013764
  7.2 154.7 %all-reduce.5.cloned.1.call-start = ((), (), s32[]{:S(2)}) async-start(), calls=%async_computation | async-start | bytes 1351680
  11.0 1.9 copy-start.1
  11.0 1.9 copy-start.2
  11.0 1.9 copy-start.3
  12.9 1.5 copy-start.4
Sparse Core Ops, SparseCore 0:
  17.9 143.9 all-reduce.4
where the time goes:
time: 372 us; the launch traced here: 368 us
  blocking collectives  251 us (67%)
  waiting for transfers between devices  89.1 us (24%)
  between operations  15.4 us (4%)
  other arithmetic  5.8 us (2%)
  matrix products  3.74 us (1%)
    psum x1, blocking collectives, reduce_bucket(): return lax.psum(owned, 'rep')  198 us
    unnamed x2, waiting for transfers between devices  89.1 us
    unnamed x1, blocking collectives  52.2 us
  transfers between devices with their start and end apart: 1, of which 1 were waited for; matrix products, arithmetic and copies ran while one was open for 0% of the time, Pallas kernels for 0%

commit v1 on v0

--- a/solution.py
+++ b/solution.py
@@ -1,7 +1,12 @@
 import jax
 import jax.numpy as jnp
 from jax import lax
+from jax.sharding import Mesh
 from jax.sharding import PartitionSpec as P
+
+LANES = 128
+SHARD = ("xl", "y")
+HOLDERS = ("z4", "z3", "xh", "core", "xl", "y")
 
 
 def token_weights(lengths, masked):
@@ -21,9 +26,21 @@
     return (live_rows, live_rows * (1.0 - masked_f) * token_scale)
 
 
-def reduce_bucket(flat_sum):
-    owned = lax.psum_scatter(flat_sum, "shard", scatter_dimension=0, tiled=True)
-    return lax.psum(owned, "rep")
+def exchange_sum(block, axes, count):
+    sent = jnp.broadcast_to(block[None], (count, *block.shape))
+    return lax.all_to_all(sent, axes, 0, 0, tiled=True)
+
+
+def reduce_pieces(pieces):
+    half = pieces.shape[1] // 2
+    core = lax.axis_index("core")
+    kept = lax.dynamic_slice_in_dim(pieces, core * half, half, 1)
+    given = lax.dynamic_slice_in_dim(pieces, (1 - core) * half, half, 1)
+    pair = kept + lax.ppermute(given, "core", [(0, 1), (1, 0)])
+    owned = jnp.sum(lax.all_to_all(pair, SHARD, 0, 0, tiled=True), axis=0)
+    far = jnp.sum(exchange_sum(owned, "z4", 4), axis=0)
+    near = exchange_sum(far, ("z3", "xh", "core"), 12)
+    return jnp.sum(near.reshape(6, 2, half, LANES), axis=0).reshape(-1)
 
 
 def embedding_sums(onehot, weight, resid_cot, normed_cot, normed, inv_std, ln_gain):
@@ -39,7 +56,7 @@
 
 def on_device(seq_lengths, token_ids, masked, embed_table, ln_gain, grad_resid, grad_normed):
     live_rows, weight = token_weights(seq_lengths[0], masked)
-    vocab_size = embed_table.shape[0]
+    vocab_size, width = embed_table.shape
     onehot = (token_ids[:, None] == jnp.arange(vocab_size, dtype=jnp.int32)[None, :]).astype(
         jnp.bfloat16
     )
@@ -58,22 +75,35 @@
             jnp.sum(normed_cot, axis=0),
         ]
     )
-    layer_owned = reduce_bucket(layer_sums.reshape(-1))
     embed_sums = embedding_sums(onehot, weight, resid_cot, normed_cot, normed, inv_std, ln_gain)
-    return (layer_owned, reduce_bucket(embed_sums.reshape(-1)))
+    embed_part = vocab_size * width // 16
+    layer_part = 3 * width // 16
+    rows = -(-(embed_part + layer_part) // (LANES * 16)) * 16
+    pad = rows * LANES - embed_part - layer_part
+    pieces = jnp.concatenate(
+        [
+            embed_sums.reshape(16, embed_part),
+            layer_sums.reshape(16, layer_part),
+            jnp.zeros((16, pad), jnp.float32),
+        ],
+        axis=1,
+    ).reshape(16, rows, LANES)
+    mine = reduce_pieces(pieces)
+    return (mine[embed_part : embed_part + layer_part], mine[:embed_part])
 
 
 def solution(mesh):
+    fine = Mesh(mesh.devices.reshape(4, 3, 2, 2, 2, 8), HOLDERS)
     in_specs = (
-        P(("rep", "shard"), None),
-        P(("rep", "shard")),
-        P(("rep", "shard")),
+        P(HOLDERS, None),
+        P(HOLDERS),
+        P(HOLDERS),
         P(),
         P(),
-        P(("rep", "shard"), None),
-        P(("rep", "shard"), None),
+        P(HOLDERS, None),
+        P(HOLDERS, None),
     )
-    out_specs = (P("shard"), P("shard"))
+    out_specs = (P(SHARD), P(SHARD))
     return jax.shard_map(
-        on_device, mesh=mesh, in_specs=in_specs, out_specs=out_specs, check_vma=False
+        on_device, mesh=fine, in_specs=in_specs, out_specs=out_specs, check_vma=False
     )

time: 372 us -> 78.1 us (0.21)
  blocking collectives: 251 us -> 51.3 us
  waiting for transfers between devices: 89.1 us -> 1.32 us
  between operations: 15.4 us -> 0.81 us
  starting transfers between devices: 0.04 us -> 12.4 us
    psum x1 -> x0, blocking collectives: 198 us -> none  [reduce_bucket(): return lax.psum(owned, 'rep')]
    unnamed x2 -> x0, waiting for transfers between devices: 89.1 us -> none
    unnamed x1 -> x0, blocking collectives: 52.2 us -> none
    all_to_all x0 -> x3, blocking collectives: none -> 51.3 us  [the longest x2 37.4 us: exchange_sum(): return lax.all_to_all(sent, axes, 0, 0, tiled=True)]
    ppermute x0 -> x1, starting transfers between devices: none -> 12.4 us  [reduce_pieces(): pair = kept + lax.ppermute(given, 'core', [(0, 1), (1, 0)])]
where the time goes in v1:
time: 78.1 us; the launch traced here: 77.8 us
  blocking collectives  51.3 us (66%)
  starting transfers between devices  12.4 us (16%)
  other arithmetic  5.93 us (8%)
  matrix products  3.71 us (5%)
  local copies, waits for them, and re-layouts  2.3 us (3%)
  waiting for transfers between devices  1.32 us (2%)
  between operations  0.81 us (1%)
    all_to_all x2, blocking collectives, exchange_sum(): return lax.all_to_all(sent, axes, 0, 0, tiled=True)  37.4 us
    all_to_all x1, blocking collectives, reduce_pieces(): owned = jnp.sum(lax.all_to_all(pair, SHARD, 0, 0, tiled=True), axis=0)  13.9 us
    ppermute x1, starting transfers between devices, reduce_pieces(): pair = kept + lax.ppermute(given, 'core', [(0, 1), (1, 0)])  12.4 us
    dot_general x1, matrix products, embedding_sums(): jnp.dot(onehot.astype(jnp.float32).T, flowing, precision=lax.Precision.HI...  2.27 us
  transfers between devices with their start and end apart: 1, of which 1 were waited for; matrix products, arithmetic and copies ran while one was open for 0% of the time, Pallas kernels for 0%

profile of v1, /device:TPU:1, one launch (start us, length us, event | category | flops | bytes accessed | tf_op | source)
XLA Modules:
  0.0 77.8 jit_solution(16514872670775684897)
XLA Ops:
  0.6 0.0 copy-start
  0.6 0.9 %reduce-window.4 = s32[2,1]{0,1:T(1,128)S(1)} reduce-window(s32[2,1]{0,1:T(1,128)} %bitcast.33, s32[]{:T(128)} %constant.12.clone.1), window={size=2x1 pad=1_0x0_0}, to_apply=%region_0.0 | reduce-window | flops 2 | bytes 20 | tf_op jit(solution)/shard_map/reduce-window
  1.5 0.7 fusion.21
  2.2 0.7 convert_element_type.20
  2.8 0.2 convert_reduce_fusion
  3.0 0.7 divide_bitcast_fusion
  3.7 0.1 select_reduce_fusion
  3.8 0.7 multiply_multiply_fusion
  4.4 0.0 copy-done
  4.5 0.0 copy-start.1
  4.5 0.0 copy-start.2
  4.5 0.0 copy-start.3
  4.5 1.4 %fusion.22 = (f32[128]{0:T(128)S(1)}, f32[128,5120]{1,0:T(8,128)S(1)}) fusion(f32[128]{0:T(128)S(1)} %multiply_multiply_fusion, bf16[33,5120]{1,0:T(8,128)(2,1)S(1)} %copy-done, s32[128]{0:T(128)} %param.8), kind=kOutput, calls=%fused_computation.44 | convolution fusion | flops 44568576 | bytes 2960896 | tf_op jit(solution)/shard_map/dot_general | solution.py:63
  5.9 0.4 multiply_reduce_fusion.2
  6.3 0.0 copy-done.1
  6.4 0.0 copy-done.2
  6.4 0.0 copy-done.3
  6.4 0.0 copy-start.4
  6.4 1.5 %multiply_reduce_fusion = (f32[5120]{0:T(1024)S(1)}, f32[128]{0:T(128)S(1)}, f32[128]{0:T(128)S(1)}, f32[5120]{0:T(1024)S(1)}, f32[5120]{0:T(1024)S(1)}) fusion(bf16[128,5120]{1,0:T(8,128)(2,1)S(1)} %copy-done.1, f32[128,5120]{1,0:T(8,128)S(1)} %get-tuple-element.10, f32[128]{0:T(128)S(1)} %add_rsqrt_fusion, f32[128]{0:T(128)S(1)} %broadcast_multiply_fusion.2, ...), kind=kLoop, calls=%fused_computation.1 | loop fusion | flops 9159424 | bytes 5327360 | tf_op jit(solution)/shard_map/reduce_sum | solution.py:74
  7.9 0.0 copy-done.4
  7.9 2.3 %fusion = f32[33,5120]{1,0:T(8,128)S(1)} fusion(bf16[128,5120]{1,0:T(8,128)(2,1)S(1)} %copy-done.1, bf16[128,5120]{1,0:T(8,128)(2,1)S(1)} %copy-done.2, f32[128,5120]{1,0:T(8,128)S(1)} %get-tuple-element.10, f32[128]{0:T(128)S(1)} %get-tuple-element.11, f32[128]{0:T(128)S(1)} %get-tuple-element.12, f32[5120]{0:T(1024)S(1)} %copy-done.3, ...), kind=kOutput, calls=%fused_computation.2 | convolution fusion | flops 268046464 | bytes 5942784 | tf_op jit(solution)/shard_map/dot_general | solution.py:54
  10.2 0.5 reshape.59
  10.8 0.1 pad_maximum_fusion
  10.8 0.1 reshape.60
  11.0 0.1 concatenate.3
  11.1 0.2 copy.9
  11.3 12.4 %collective-permute-start = (f32[16,48,128]{2,1,0:T(8,128)S(1)}, f32[16,48,128]{2,1,0:T(8,128)S(1)}, u32[]{:S(2)}, u32[]{:S(2)}) collective-permute-start(f32[16,48,128]{2,1,0:T(8,128)S(1)} %constant_dynamic-slice_fusion), channel_id=1, source_target_pairs={{0,16},{16,0},{1,17},{17,1},{2,18},{18,2},{3,19},{19,3},{4,20},{20... | collective-permute-start | bytes 1179656 | tf_op jit(solution)/shard_map/ppermute | solution.py:39
  23.7 1.3 %collective-permute-done = f32[16,48,128]{2,1,0:T(8,128)S(1)} collective-permute-done((f32[16,48,128]{2,1,0:T(8,128)S(1)}, f32[16,48,128]{2,1,0:T(8,128)S(1)}, u32[]{:S(2)}, u32[]{:S(2)}) %collective-permute-start) | collective-permute-done | bytes 393248 | tf_op jit(solution)/shard_map/ppermute | solution.py:39
  25.0 0.1 dynamic-slice_add_fusion
  25.1 13.9 %all_to_all.15 = f32[16,48,128]{2,1,0:T(8,128)S(1)} all-to-all(f32[16,48,128]{2,1,0:T(8,128)S(1)} %dynamic-slice_add_fusion), channel_id=1, replica_groups=mesh['z4'=4,'z3'=3,'xh'=2,'core'=2,'xl'=2,'y'=8] {'xl','y'}, dimensions={0} | all-to-all | bytes 786432 | tf_op jit(solution)/shard_map/all_to_all | solution.py:40
  39.0 19.6 %all_to_all.16 = f32[4,48,128]{2,1,0:T(8,128)S(1)} all-to-all(f32[4,48,128]{2,1,0:T(8,128)S(1)} %broadcast_in_dim.7), channel_id=1, replica_groups=mesh['z4'=4,'z3'=3,'xh'=2,'core'=2,'xl'=2,'y'=8] {'z4'}, dimensions={0} | all-to-all | bytes 196608 | tf_op jit(solution)/shard_map/all_to_all | solution.py:31
  58.7 17.8 %all_to_all.17 = f32[12,48,128]{2,1,0:T(8,128)S(1)} all-to-all(f32[12,48,128]{2,1,0:T(8,128)S(1)} %broadcast_in_dim.8), channel_id=1, replica_groups=mesh['z4'=4,'z3'=3,'xh'=2,'core'=2,'xl'=2,'y'=8] {'z3','xh','core'}, dimensions={0} | all-to-all | bytes 589824 | tf_op jit(solution)/shard_map/all_to_all | solution.py:31
  76.5 0.7 slice.8
  77.2 0.6 slice.9
  (10 shorter events, 0.1 us)
Async XLA Ops:
  0.6 3.8 %copy-start = (bf16[33,5120]{1,0:T(8,128)(2,1)S(1)}, bf16[33,5120]{1,0:T(8,128)(2,1)}, u32[]{:S(2)}) copy-start(bf16[33,5120]{1,0:T(8,128)(2,1)} %param.10) | copy-start | bytes 1013764
  4.5 1.9 %copy-start.1 = (bf16[128,5120]{1,0:T(8,128)(2,1)S(1)}, bf16[128,5120]{1,0:T(8,128)(2,1)}, u32[]{:S(2)}) copy-start(bf16[128,5120]{1,0:T(8,128)(2,1)} %param.13) | copy-start | bytes 3932164
  4.5 1.9 %copy-start.2 = (bf16[128,5120]{1,0:T(8,128)(2,1)S(1)}, bf16[128,5120]{1,0:T(8,128)(2,1)}, u32[]{:S(2)}) copy-start(bf16[128,5120]{1,0:T(8,128)(2,1)} %param.12) | copy-start | bytes 3932164
  4.5 1.9 %copy-start.3 = (f32[5120]{0:T(1024)S(1)}, f32[5120]{0:T(1024)}, u32[]{:S(2)}) copy-start(f32[5120]{0:T(1024)} %param.11) | copy-start | bytes 61444
  6.4 1.5 %copy-start.4 = (s32[128]{0:T(128)S(1)}, s32[128]{0:T(128)}, u32[]{:S(2)}) copy-start(s32[128]{0:T(128)} %param.8) | copy-start | bytes 1540
  11.3 13.8 %collective-permute-start = (f32[16,48,128]{2,1,0:T(8,128)S(1)}, f32[16,48,128]{2,1,0:T(8,128)S(1)}, u32[]{:S(2)}, u32[]{:S(2)}) collective-permute-start(f32[16,48,128]{2,1,0:T(8,128)S(1)} %constant_dynamic-slice_fusion), channel_id=1, source_target_pairs={{0,16},{16,0},{1,17},{17,1},{2,18},{18,2},{3,19},{19,3},{4,20},{20... | collective-permute-start | bytes 1179656 | tf_op jit(solution)/shard_map/ppermute | solution.py:39

commit v2 on v0

v2 whole, which is shorter than its diff:
```python
import jax
import jax.numpy as jnp
from jax import lax
from jax.experimental import pallas as pl
from jax.experimental.pallas import tpu as pltpu
from jax.sharding import Mesh
from jax.sharding import PartitionSpec as P

LANES = 128
SUBLANES = 8
EPS = 1e-05
SHRINK = 2.0**-8
WIDTH_STEP = 512
VOCAB_USED = 32
OWNERS = 16
QUARTERS = 4
PIECE = 24
HOLDERS = ("z", "xh", "core", "xl", "y")


def token_rows(lengths_ref, masked_ref):
    masked = masked_ref[...].astype(jnp.float32)
    position = lax.broadcasted_iota(jnp.int32, masked.shape, 1)
    first, second = lengths_ref[0, 0], lengths_ref[0, 1]
    members = (position < first, (position >= first) & (position < first + second))
    scale = jnp.zeros_like(masked)
    for member, length in zip(members, (first, second)):
        length_f = jnp.full((1, 1), length, jnp.int32).astype(jnp.float32)
        count = jnp.sum(jnp.where(member, masked, 0.0), axis=1, keepdims=True)
        factor = 0.88 / jnp.maximum(1.0 - count / length_f, 0.5)
        scale = jnp.where(member, factor, scale)
    live = jnp.where(members[0] | members[1], 1.0, 0.0)
    return live, live * (1.0 - masked) * scale


def split3(value):
    high = value.astype(jnp.bfloat16)
    rest = value - high.astype(jnp.float32)
    mid = rest.astype(jnp.bfloat16)
    low = (rest - mid.astype(jnp.float32)).astype(jnp.bfloat16)
    return [high, mid, low]


def sum3(parts, at):
    n = VOCAB_USED
    return parts[at : at + n] + parts[at + n : at + 2 * n] + parts[at + 2 * n : at + 3 * n]


def lane_fold(value):
    total = value[:, :LANES]
    for at in range(LANES, value.shape[1], LANES):
        total = total + value[:, at : at + LANES]
    return total


def sums_kernel(
    lengths_ref, ids_ref, masked_ref, table_ref, gain_ref, resid_ref, normed_ref,
    given_ref, kept_ref, total_ref, flat_ref,
):
    width = table_ref.shape[1]
    blocks = width // LANES
    live, weight = token_rows(lengths_ref, masked_ref)
    n, slots = VOCAB_USED, weight.shape[1]
    small = table_ref[0:n, :].astype(jnp.float32) * SHRINK
    mean = jnp.sum(small, axis=1, keepdims=True) / width
    small = small - mean
    spread = jnp.sum(small * small, axis=1, keepdims=True) / width
    variance = jnp.minimum(spread * SHRINK**-2, 1e38)
    unit = lax.rsqrt(variance + EPS)
    unscaled = (variance + EPS) * unit

    hit = ids_ref[...] == lax.broadcasted_iota(jnp.int32, (n, slots), 0)
    weighted = jnp.where(hit, weight, 0.0)
    through = weighted * lax.rsqrt(weight * weight * variance + EPS)
    ratio = through * unscaled
    row = lax.broadcasted_iota(jnp.int32, (16, slots), 0)
    alive = jnp.where(row == 0, live, 0.0).astype(jnp.bfloat16)
    left_resid = jnp.concatenate([*split3(weighted), alive], axis=0)
    left_normed = jnp.concatenate(
        [*split3(through), *split3(through * ratio * ratio), alive], axis=0
    )

    mean_sum = jnp.zeros((n, LANES), jnp.float32)
    slope_sum = jnp.zeros((n, LANES), jnp.float32)
    for at in range(0, width, WIDTH_STEP):
        columns = slice(at, at + WIDTH_STEP)
        from_resid = jnp.dot(left_resid, resid_ref[:, columns], preferred_element_type=jnp.float32)
        from_normed = jnp.dot(
            left_normed, normed_ref[:, columns], preferred_element_type=jnp.float32
        )
        gain = gain_ref[:, columns]
        centered = table_ref[0:n, columns].astype(jnp.float32) * SHRINK - mean
        centered = centered * SHRINK**-1
        passed = sum3(from_normed, 0)
        gained = passed * gain
        mean_sum += lane_fold(gained)
        slope_sum += lane_fold(centered * unit * gain * sum3(from_normed, 3 * n))
        total_ref[:, columns] = sum3(from_resid, 0) + gained
        gain_grad = jnp.sum(centered * passed, axis=0, keepdims=True)
        row = lax.broadcasted_iota(jnp.int32, (SUBLANES, WIDTH_STEP), 0)
        layer = jnp.where(
            row == 1,
            from_resid[3 * n : 3 * n + 1],
            jnp.where(row == 2, gain_grad, jnp.where(row == 3, from_normed[6 * n : 6 * n + 1], 0.0)),
        )
        for k in range(WIDTH_STEP // LANES):
            at_row = n * blocks + at // LANES + k
            flat_ref[pl.ds(at_row, SUBLANES, stride=blocks), :] = layer[
                :, k * LANES : (k + 1) * LANES
            ]
    mean_sum = jnp.sum(mean_sum, axis=1, keepdims=True) / width
    slope = jnp.sum(slope_sum, axis=1, keepdims=True) / width * unit
    for k in range(blocks):
        columns = slice(k * LANES, (k + 1) * LANES)
        centered = table_ref[0:n, columns].astype(jnp.float32) * SHRINK - mean
        result = total_ref[:, columns] - mean_sum - centered * SHRINK**-1 * slope
        for tile in range(n // SUBLANES):
            rows = slice(tile * SUBLANES, (tile + 1) * SUBLANES)
            flat_ref[pl.ds(tile * SUBLANES * blocks + k, SUBLANES, stride=blocks), :] = result[rows]

    layer_row = (n + 1) * blocks

    def write(out_ref, core):
        for owner in range(OWNERS):
            for tile in range(PIECE * QUARTERS // SUBLANES):
                quarter, inner = divmod(tile, PIECE // SUBLANES)
                if quarter % 2 != core:
                    continue
                if tile == 0:
                    start = layer_row + owner * 15 // 2
                else:
                    start = owner * 165 // 2 + (tile - 1) * SUBLANES
                out_ref[quarter // 2 * OWNERS + owner, pl.ds(inner * SUBLANES, SUBLANES), :] = (
                    flat_ref[pl.ds(start, SUBLANES), :]
                )

    core = lax.axis_index("core")
    for value in range(2):

        @pl.when(core == value)
        def _():
            write(kept_ref, value)
            write(given_ref, 1 - value)


def local_sums(lengths, ids, masked, table, gain, resid, normed):
    width = table.shape[1]
    vmem = pl.BlockSpec(memory_space=pltpu.VMEM)
    smem = pl.BlockSpec(memory_space=pltpu.SMEM)
    out = jax.ShapeDtypeStruct((2 * OWNERS, PIECE, LANES), jnp.float32)
    return pl.pallas_call(
        sums_kernel,
        out_shape=(out, out),
        in_specs=[smem] + [vmem] * 6,
        out_specs=(vmem, vmem),
        scratch_shapes=[
            pltpu.VMEM((VOCAB_USED, width), jnp.float32),
            pltpu.VMEM(((VOCAB_USED + SUBLANES) * width // LANES, LANES), jnp.float32),
        ],
        compiler_params=pltpu.CompilerParams(vmem_limit_bytes=32 * 1024 * 1024),
        name="local_sums",
    )(lengths, ids[None], masked[None], table, gain[None], resid, normed)


def to_all(block, axes, count):
    sent = jnp.broadcast_to(block[None], (count, *block.shape))
    return lax.all_to_all(sent, axes, 0, 0, tiled=True)


def on_device(lengths, ids, masked, table, gain, resid, normed):
    given, kept = local_sums(lengths, ids, masked, table, gain, resid, normed)
    pair = kept + lax.ppermute(given, "core", [(0, 1), (1, 0)])
    piece = jnp.sum(lax.all_to_all(pair, ("xh", "xl", "y"), 0, 0, tiled=True), axis=0)
    piece = jnp.sum(to_all(piece, "z", 12), axis=0)
    owned = to_all(piece, ("xh", "core"), QUARTERS).reshape(-1)
    shift = (lax.axis_index("y") & 1) * (LANES // 2)
    layer = lax.dynamic_slice_in_dim(owned, shift, 3 * table.shape[1] // OWNERS)
    embed = lax.dynamic_slice_in_dim(
        owned, SUBLANES * LANES + shift, table.shape[0] * table.shape[1] // OWNERS
    )
    return layer, embed


def solution(mesh):
    fine = Mesh(mesh.devices.reshape(12, 2, 2, 2, 8), HOLDERS)
    in_specs = (
        P(HOLDERS, None),
        P(HOLDERS),
        P(HOLDERS),
        P(),
        P(),
        P(HOLDERS, None),
        P(HOLDERS, None),
    )
    owners = P(("xl", "y"))
    return jax.shard_map(
        on_device, mesh=fine, in_specs=in_specs, out_specs=(owners, owners), check_vma=False
    )
```

time: 372 us -> 76.2 us (0.20)
  blocking collectives: 251 us -> 37.7 us
  waiting for transfers between devices: 89.1 us -> 6.05 us
  starting transfers between devices: 0.04 us -> 20.5 us
  between operations: 15.4 us -> 0.68 us
  other arithmetic: 5.8 us -> 0.1 us
  local copies, waits for them, and re-layouts: 3.25 us -> 8.32 us
  matrix products: 3.74 us -> 0 us
    psum x1 -> x0, blocking collectives: 198 us -> none  [reduce_bucket(): return lax.psum(owned, 'rep')]
    unnamed x2 -> x0, waiting for transfers between devices: 89.1 us -> none
    unnamed x1 -> x0, blocking collectives: 52.2 us -> none
    all_to_all x0 -> x2, blocking collectives: none -> 37.7 us  [the longest x1 22.4 us: to_all(): return lax.all_to_all(sent, axes, 0, 0, tiled=True)]
    ppermute x0 -> x1, starting transfers between devices: none -> 12.4 us  [on_device(): pair = kept + lax.ppermute(given, 'core', [(0, 1), (1, 0)])]
    all_to_all x0 -> x1, starting transfers between devices: none -> 8.03 us  [to_all(): return lax.all_to_all(sent, axes, 0, 0, tiled=True)]
    all_to_all x0 -> x1, waiting for transfers between devices: none -> 4.72 us  [to_all(): return lax.all_to_all(sent, axes, 0, 0, tiled=True)]
    unnamed x13 -> x14, local copies, waits for them, and re-layouts: 2.26 us -> 6.32 us
  transfers between devices with their start and end apart: 1 -> 2, of which waited for: 1 -> 2; matrix products, arithmetic and copies ran while one was open for 0% -> 0% of each run, Pallas kernels for 0% -> 0%
where the time goes in v2:
time: 76.2 us; the launch traced here: 75.4 us
  blocking collectives  37.7 us (49%)
  starting transfers between devices  20.5 us (27%)
  local copies, waits for them, and re-layouts  8.32 us (11%)
  waiting for transfers between devices  6.05 us (8%)
  Pallas kernels  2.1 us (3%)
    all_to_all x1, blocking collectives, to_all(): return lax.all_to_all(sent, axes, 0, 0, tiled=True)  22.4 us
    all_to_all x1, blocking collectives, on_device(): lax.all_to_all(pair, ('xh', 'xl', 'y'), 0, 0, tiled=True)  15.3 us
    ppermute x1, starting transfers between devices, on_device(): pair = kept + lax.ppermute(given, 'core', [(0, 1), (1, 0)])  12.4 us
    all_to_all x1, starting transfers between devices, to_all(): return lax.all_to_all(sent, axes, 0, 0, tiled=True)  8.03 us
    unnamed x14, local copies, waits for them, and re-layouts  6.32 us
    all_to_all x1, waiting for transfers between devices, to_all(): return lax.all_to_all(sent, axes, 0, 0, tiled=True)  4.72 us
    pallas_call x1, Pallas kernels, local_sums(): pl.pallas_call(sums_kernel, out_shape=(out, out), in_specs=[smem] + [vmem...  2.1 us
  transfers between devices with their start and end apart: 2, of which 2 were waited for; matrix products, arithmetic and copies ran while one was open for 0% of the time, Pallas kernels for 0%

profile of v2, /device:TPU:1, one launch (start us, length us, event | category | flops | bytes accessed | tf_op | source)
XLA Modules:
  0.0 75.4 jit_solution(1603387251109552248)
XLA Ops:
  0.6 0.0 copy-start
  0.6 1.3 %copy-done = bf16[128,5120]{1,0:T(8,128)(2,1)S(1)} copy-done((bf16[128,5120]{1,0:T(8,128)(2,1)S(1)}, bf16[128,5120]{1,0:T(8,128)(2,1)}, u32[]{:S(2)}) %copy-start) | copy-done | bytes 1310744
  1.9 0.0 copy-start.1
  2.0 1.3 %copy-done.1 = bf16[128,5120]{1,0:T(8,128)(2,1)S(1)} copy-done((bf16[128,5120]{1,0:T(8,128)(2,1)S(1)}, bf16[128,5120]{1,0:T(8,128)(2,1)}, u32[]{:S(2)}) %copy-start.1) | copy-done | bytes 1310744
  3.3 0.0 copy-start.2
  3.3 1.0 %copy-done.2 = bf16[33,5120]{1,0:T(8,128)(2,1)S(1)} copy-done((bf16[33,5120]{1,0:T(8,128)(2,1)S(1)}, bf16[33,5120]{1,0:T(8,128)(2,1)}, u32[]{:S(2)}) %copy-start.2) | copy-done | bytes 337944
  4.3 0.0 copy-start.3
  4.3 0.7 copy-done.3
  5.0 0.0 copy-start.4
  5.0 0.7 copy-done.4
  5.7 0.0 copy-start.5
  5.7 0.7 copy-done.5
  6.3 0.0 copy-start.6
  6.3 0.7 copy-done.6
  7.0 2.1 %local_sums.1 = (f32[32,24,128]{2,1,0:T(8,128)S(1)}, f32[32,24,128]{2,1,0:T(8,128)S(1)}) custom-call(s32[1,2]{1,0:T(1,128)S(1)} %copy-done.4, s32[1,128]{1,0:T(1,128)S(1)} %bitcast.5, s32[1,128]{1,0:T(1,128)S(1)} %bitcast.6, bf16[33,5120]{1,0:T(8,128)(2,1)S(1)} %copy-done.2, f32[1,5120]{1,0:T(1,128)S(1)} %bitcast.4, bf16[128,5120]{1,0:T(8,128)(2,1)S(1)} %copy-done, ...), custom_call_target="tpu_custom_call" | custom-call | tf_op jit(solution)/shard_map/local_sums/pallas_call | solution.py:151
  9.1 12.4 %collective-permute-start = (f32[32,24,128]{2,1,0:T(8,128)S(1)}, f32[32,24,128]{2,1,0:T(8,128)S(1)}, u32[]{:S(2)}, u32[]{:S(2)}) collective-permute-start(f32[32,24,128]{2,1,0:T(8,128)S(1)} %get-tuple-element.5), channel_id=1, source_target_pairs={{0,16},{16,0},{1,17},{17,1},{2,18},{18,2},{3,19},{19,3},{4,20},{20... | collective-permute-start | bytes 1179656 | tf_op jit(solution)/shard_map/ppermute | solution.py:172
  21.5 1.3 %collective-permute-done = f32[32,24,128]{2,1,0:T(8,128)S(1)} collective-permute-done((f32[32,24,128]{2,1,0:T(8,128)S(1)}, f32[32,24,128]{2,1,0:T(8,128)S(1)}, u32[]{:S(2)}, u32[]{:S(2)}) %collective-permute-start) | collective-permute-done | bytes 393248 | tf_op jit(solution)/shard_map/ppermute | solution.py:172
  22.9 15.3 %all_to_all.15 = f32[32,24,128]{2,1,0:T(8,128)S(1)} all-to-all(f32[32,24,128]{2,1,0:T(8,128)S(1)} %add.11), channel_id=1, replica_groups=mesh['z'=12,'xh'=2,'core'=2,'xl'=2,'y'=8] {'xh','xl','y'}, dimensions={0} | all-to-all | bytes 786432 | tf_op jit(solution)/shard_map/all_to_all | solution.py:173
  38.2 22.4 %all_to_all.16 = f32[12,24,128]{2,1,0:T(8,128)S(1)} all-to-all(f32[12,24,128]{2,1,0:T(8,128)S(1)} %broadcast_in_dim.24), channel_id=1, replica_groups=mesh['z'=12,'xh'=2,'core'=2,'xl'=2,'y'=8] {'z'}, dimensions={0} | all-to-all | bytes 294912 | tf_op jit(solution)/shard_map/all_to_all | solution.py:167
  60.6 0.6 broadcast_in_dim.25
  61.2 8.0 %all-to-all-start.2 = ((f32[4,24,128]{2,1,0:T(8,128)}), f32[4,24,128]{2,1,0:T(8,128)S(1)}, u32[]{:S(2)}, u32[]{:S(2)}) async-start(f32[4,24,128]{2,1,0:T(8,128)} %broadcast_in_dim.25), calls=%async_computation.2 | async-start | bytes 98304 | tf_op jit(solution)/shard_map/all_to_all | solution.py:167
  69.3 4.7 %all-to-all-done.2 = f32[4,24,128]{2,1,0:T(8,128)S(1)} async-done(((f32[4,24,128]{2,1,0:T(8,128)}), f32[4,24,128]{2,1,0:T(8,128)S(1)}, u32[]{:S(2)}, u32[]{:S(2)}) %all-to-all-start.2) | async-done | bytes 49184 | tf_op jit(solution)/shard_map/all_to_all | solution.py:167
  74.0 0.7 dynamic_slice.6
  74.7 0.7 dynamic_slice.7
  (4 shorter events, 0.1 us)
Async XLA Ops:
  0.6 1.3 %copy-start = (bf16[128,5120]{1,0:T(8,128)(2,1)S(1)}, bf16[128,5120]{1,0:T(8,128)(2,1)}, u32[]{:S(2)}) copy-start(bf16[128,5120]{1,0:T(8,128)(2,1)} %resid_ref.1) | copy-start | bytes 3932164
  1.9 1.3 %copy-start.1 = (bf16[128,5120]{1,0:T(8,128)(2,1)S(1)}, bf16[128,5120]{1,0:T(8,128)(2,1)}, u32[]{:S(2)}) copy-start(bf16[128,5120]{1,0:T(8,128)(2,1)} %normed_ref.1) | copy-start | bytes 3932164
  3.3 1.0 %copy-start.2 = (bf16[33,5120]{1,0:T(8,128)(2,1)S(1)}, bf16[33,5120]{1,0:T(8,128)(2,1)}, u32[]{:S(2)}) copy-start(bf16[33,5120]{1,0:T(8,128)(2,1)} %table_ref.1) | copy-start | bytes 1013764
  4.3 0.7 copy-start.3
  5.0 0.7 copy-start.4
  5.7 0.7 copy-start.5
  6.3 0.7 copy-start.6
  9.1 13.8 %collective-permute-start = (f32[32,24,128]{2,1,0:T(8,128)S(1)}, f32[32,24,128]{2,1,0:T(8,128)S(1)}, u32[]{:S(2)}, u32[]{:S(2)}) collective-permute-start(f32[32,24,128]{2,1,0:T(8,128)S(1)} %get-tuple-element.5), channel_id=1, source_target_pairs={{0,16},{16,0},{1,17},{17,1},{2,18},{18,2},{3,19},{19,3},{4,20},{20... | collective-permute-start | bytes 1179656 | tf_op jit(solution)/shard_map/ppermute | solution.py:172
  61.2 12.7 %all-to-all-start.2 = ((f32[4,24,128]{2,1,0:T(8,128)}), f32[4,24,128]{2,1,0:T(8,128)S(1)}, u32[]{:S(2)}, u32[]{:S(2)}) async-start(f32[4,24,128]{2,1,0:T(8,128)} %broadcast_in_dim.25), calls=%async_computation.2 | async-start | bytes 98304 | tf_op jit(solution)/shard_map/all_to_all | solution.py:167

commit v3 on v2

--- a/solution.py
+++ b/solution.py
@@ -11,6 +11,7 @@
 EPS = 1e-05
 SHRINK = 2.0**-8
 WIDTH_STEP = 512
+COPY_STEP = 1024
 VOCAB_USED = 32
 OWNERS = 16
 QUARTERS = 4
@@ -54,9 +55,39 @@
 
 
 def sums_kernel(
+    lengths_hbm, ids_hbm, masked_hbm, table_hbm, gain_hbm, resid_hbm, normed_hbm,
+    given_ref, kept_ref,
     lengths_ref, ids_ref, masked_ref, table_ref, gain_ref, resid_ref, normed_ref,
-    given_ref, kept_ref, total_ref, flat_ref,
+    total_ref, flat_ref, small_sem, resid_sem, normed_sem,
 ):
+    small_copies = [
+        pltpu.make_async_copy(source, target, small_sem.at[i])
+        for i, (source, target) in enumerate(
+            (
+                (table_hbm, table_ref),
+                (lengths_hbm, lengths_ref),
+                (masked_hbm, masked_ref),
+                (ids_hbm, ids_ref),
+                (gain_hbm, gain_ref),
+            )
+        )
+    ]
+    large_copies = []
+    for i in range(table_ref.shape[1] // COPY_STEP):
+        columns = pl.ds(i * COPY_STEP, COPY_STEP)
+        large_copies.append(
+            [
+                pltpu.make_async_copy(source.at[:, columns], target.at[:, columns], sem.at[i])
+                for source, target, sem in (
+                    (resid_hbm, resid_ref, resid_sem),
+                    (normed_hbm, normed_ref, normed_sem),
+                )
+            ]
+        )
+    for copy in small_copies + sum(large_copies, []):
+        copy.start()
+    for copy in small_copies:
+        copy.wait()
     width = table_ref.shape[1]
     blocks = width // LANES
     live, weight = token_rows(lengths_ref, masked_ref)
@@ -83,6 +114,9 @@
     mean_sum = jnp.zeros((n, LANES), jnp.float32)
     slope_sum = jnp.zeros((n, LANES), jnp.float32)
     for at in range(0, width, WIDTH_STEP):
+        if at % COPY_STEP == 0:
+            for copy in large_copies[at // COPY_STEP]:
+                copy.wait()
         columns = slice(at, at + WIDTH_STEP)
         from_resid = jnp.dot(left_resid, resid_ref[:, columns], preferred_element_type=jnp.float32)
         from_normed = jnp.dot(
@@ -146,20 +180,67 @@
 def local_sums(lengths, ids, masked, table, gain, resid, normed):
     width = table.shape[1]
     vmem = pl.BlockSpec(memory_space=pltpu.VMEM)
-    smem = pl.BlockSpec(memory_space=pltpu.SMEM)
+    hbm = pl.BlockSpec(memory_space=pltpu.HBM)
     out = jax.ShapeDtypeStruct((2 * OWNERS, PIECE, LANES), jnp.float32)
     return pl.pallas_call(
         sums_kernel,
         out_shape=(out, out),
-        in_specs=[smem] + [vmem] * 6,
+        in_specs=[hbm] * 7,
         out_specs=(vmem, vmem),
         scratch_shapes=[
+            pltpu.SMEM(lengths.shape, jnp.int32),
+            pltpu.VMEM((1, ids.shape[0]), jnp.int32),
+            pltpu.VMEM((1, ids.shape[0]), jnp.int32),
+            pltpu.VMEM(table.shape, table.dtype),
+            pltpu.VMEM((1, width), jnp.float32),
+            pltpu.VMEM(resid.shape, resid.dtype),
+            pltpu.VMEM(normed.shape, normed.dtype),
             pltpu.VMEM((VOCAB_USED, width), jnp.float32),
             pltpu.VMEM(((VOCAB_USED + SUBLANES) * width // LANES, LANES), jnp.float32),
+            pltpu.SemaphoreType.DMA((5,)),
+            pltpu.SemaphoreType.DMA((width // COPY_STEP,)),
+            pltpu.SemaphoreType.DMA((width // COPY_STEP,)),
         ],
-        compiler_params=pltpu.CompilerParams(vmem_limit_bytes=32 * 1024 * 1024),
+        compiler_params=pltpu.CompilerParams(vmem_limit_bytes=60 * 1024 * 1024),
         name="local_sums",
     )(lengths, ids[None], masked[None], table, gain[None], resid, normed)
+
+
+def own_kernel(pieces_ref, layer_ref, embed_ref):
+    half = LANES // 2
+    odd = (lax.axis_index("y") & 1) == 1
+    tiles = [
+        pieces_ref[tile * SUBLANES // PIECE, pl.ds(tile * SUBLANES % PIECE, SUBLANES), :]
+        for tile in range(PIECE * QUARTERS // SUBLANES)
+    ]
+    rolled = [pltpu.roll(tile, half, 1) for tile in tiles]
+    lane = lax.broadcasted_iota(jnp.int32, (SUBLANES, LANES), 1)
+    row = lax.broadcasted_iota(jnp.int32, (SUBLANES, LANES), 0)
+    pieces = []
+    for at, tile in enumerate(tiles):
+        after = rolled[min(at + 1, len(tiles) - 1)]
+        below = jnp.where(row == SUBLANES - 1, after[0:1], pltpu.roll(rolled[at], SUBLANES - 1, 0))
+        pieces.append(jnp.where(odd, jnp.where(lane < half, rolled[at], below), tile))
+    size = SUBLANES * LANES
+    layer_ref[...] = pieces[0].reshape(size)[: layer_ref.shape[0]]
+    for at, piece in enumerate(pieces[1:]):
+        count = min(size, embed_ref.shape[0] - at * size)
+        embed_ref[pl.ds(at * size, count)] = piece.reshape(size)[:count]
+
+
+def own_blocks(pieces, layer, embed):
+    vmem = pl.BlockSpec(memory_space=pltpu.VMEM)
+    return pl.pallas_call(
+        own_kernel,
+        out_shape=(
+            jax.ShapeDtypeStruct((layer,), jnp.float32),
+            jax.ShapeDtypeStruct((embed,), jnp.float32),
+        ),
+        in_specs=[vmem],
+        out_specs=(vmem, vmem),
+        compiler_params=pltpu.CompilerParams(vmem_limit_bytes=4 * 1024 * 1024),
+        name="own_blocks",
+    )(pieces)
 
 
 def to_all(block, axes, count):
@@ -172,13 +253,10 @@
     pair = kept + lax.ppermute(given, "core", [(0, 1), (1, 0)])
     piece = jnp.sum(lax.all_to_all(pair, ("xh", "xl", "y"), 0, 0, tiled=True), axis=0)
     piece = jnp.sum(to_all(piece, "z", 12), axis=0)
-    owned = to_all(piece, ("xh", "core"), QUARTERS).reshape(-1)
-    shift = (lax.axis_index("y") & 1) * (LANES // 2)
-    layer = lax.dynamic_slice_in_dim(owned, shift, 3 * table.shape[1] // OWNERS)
-    embed = lax.dynamic_slice_in_dim(
-        owned, SUBLANES * LANES + shift, table.shape[0] * table.shape[1] // OWNERS
-    )
-    return layer, embed
+    pieces = to_all(piece, ("xh", "core"), QUARTERS)
+    return own_blocks(
+        pieces, 3 * table.shape[1] // OWNERS, table.shape[0] * table.shape[1] // OWNERS
+    )
 
 
 def solution(mesh):

time: 76.2 us -> 71.8 us (0.942)
  blocking collectives: 37.7 us -> 50.2 us
  local copies, waits for them, and re-layouts: 8.32 us -> 0.02 us
  starting transfers between devices: 20.5 us -> 12.4 us
  waiting for transfers between devices: 6.05 us -> 1.54 us
  Pallas kernels: 2.1 us -> 5.5 us
  other arithmetic: 0.1 us -> 1.09 us
    all_to_all x1 -> x2, blocking collectives: 22.4 us -> 34.9 us  [to_all(): return lax.all_to_all(sent, axes, 0, 0, tiled=True)]
    all_to_all x1 -> x0, starting transfers between devices: 8.03 us -> none  [to_all(): return lax.all_to_all(sent, axes, 0, 0, tiled=True)]
    unnamed x14 -> x0, local copies, waits for them, and re-layouts: 6.32 us -> none
    all_to_all x1 -> x0, waiting for transfers between devices: 4.72 us -> none  [to_all(): return lax.all_to_all(sent, axes, 0, 0, tiled=True)]
    pallas_call x1 -> x2, Pallas kernels: 2.1 us -> 5.5 us  [the longest x1 4.8 us: local_sums(): pl.pallas_call(sums_kernel, out_shape=(out, out), in_specs=[hbm] * 7, out...]
    dynamic_slice x2 -> x0, local copies, waits for them, and re-layouts: 1.37 us -> none  [the longest x1 0.7 us: on_device(): lax.dynamic_slice_in_dim(owned, SUBLANES * LANES + shift, table.shape[0]...]
    add x1, other arithmetic: 0.04 us -> 1.04 us  [on_device(): pair = kept + lax.ppermute(given, 'core', [(0, 1), (1, 0)])]
  transfers between devices with their start and end apart: 2 -> 1, of which waited for: 2 -> 1; matrix products, arithmetic and copies ran while one was open for 0% -> 0% of each run, Pallas kernels for 0% -> 0%
where the time goes in v3:
time: 71.8 us; the launch traced here: 71.5 us
  blocking collectives  50.2 us (70%)
  starting transfers between devices  12.4 us (17%)
  Pallas kernels  5.5 us (8%)
  waiting for transfers between devices  1.54 us (2%)
  other arithmetic  1.09 us (2%)
    all_to_all x2, blocking collectives, to_all(): return lax.all_to_all(sent, axes, 0, 0, tiled=True)  34.9 us
    all_to_all x1, blocking collectives, on_device(): lax.all_to_all(pair, ('xh', 'xl', 'y'), 0, 0, tiled=True)  15.3 us
    ppermute x1, starting transfers between devices, on_device(): pair = kept + lax.ppermute(given, 'core', [(0, 1), (1, 0)])  12.4 us
    pallas_call x1, Pallas kernels, local_sums(): pl.pallas_call(sums_kernel, out_shape=(out, out), in_specs=[hbm] * 7, out...  4.8 us
    ppermute x1, waiting for transfers between devices, on_device(): pair = kept + lax.ppermute(given, 'core', [(0, 1), (1, 0)])  1.54 us
  transfers between devices with their start and end apart: 1, of which 1 were waited for; matrix products, arithmetic and copies ran while one was open for 0% of the time, Pallas kernels for 0%

profile of v3, /device:TPU:1, one launch (start us, length us, event | category | flops | bytes accessed | tf_op | source)
XLA Modules:
  0.0 71.5 jit_solution(14897331759564872173)
XLA Ops:
  0.6 4.8 %local_sums.1 = (f32[32,24,128]{2,1,0:T(8,128)}, f32[32,24,128]{2,1,0:T(8,128)}) custom-call(s32[1,2]{1,0:T(1,128)} %lengths_hbm.1, s32[1,128]{1,0:T(1,128)} %bitcast.4, s32[1,128]{1,0:T(1,128)} %bitcast.5, bf16[33,5120]{1,0:T(8,128)(2,1)} %table_hbm.1, f32[1,5120]{1,0:T(1,128)} %bitcast.3, bf16[128,5120]{1,0:T(8,128)(2,1)} %resid_hbm.1, ...), custom_call_target="tpu_custom_call" | custom-call | tf_op jit(solution)/shard_map/local_sums/pallas_call | solution.py:185
  5.4 12.4 %collective-permute-start = (f32[32,24,128]{2,1,0:T(8,128)}, f32[32,24,128]{2,1,0:T(8,128)S(1)}, u32[]{:S(2)}, u32[]{:S(2)}) collective-permute-start(f32[32,24,128]{2,1,0:T(8,128)} %get-tuple-element.5), channel_id=1, source_target_pairs={{0,16},{16,0},{1,17},{17,1},{2,18},{18,2},{3,19},{19,3},{4,20},{20... | collective-permute-start | bytes 1179656 | tf_op jit(solution)/shard_map/ppermute | solution.py:253
  17.9 1.5 %collective-permute-done = f32[32,24,128]{2,1,0:T(8,128)S(1)} collective-permute-done((f32[32,24,128]{2,1,0:T(8,128)}, f32[32,24,128]{2,1,0:T(8,128)S(1)}, u32[]{:S(2)}, u32[]{:S(2)}) %collective-permute-start) | collective-permute-done | bytes 393248 | tf_op jit(solution)/shard_map/ppermute | solution.py:253
  19.4 1.0 %add.3 = f32[32,24,128]{2,1,0:T(8,128)S(1)} add(f32[32,24,128]{2,1,0:T(8,128)} %get-tuple-element.4, f32[32,24,128]{2,1,0:T(8,128)S(1)} %collective-permute-done) | non-fusion elementwise | flops 98304 | bytes 1179648 | tf_op jit(solution)/shard_map/add | solution.py:253
  20.5 15.3 %all_to_all.15 = f32[32,24,128]{2,1,0:T(8,128)S(1)} all-to-all(f32[32,24,128]{2,1,0:T(8,128)S(1)} %add.3), channel_id=1, replica_groups=mesh['z'=12,'xh'=2,'core'=2,'xl'=2,'y'=8] {'xh','xl','y'}, dimensions={0} | all-to-all | bytes 786432 | tf_op jit(solution)/shard_map/all_to_all | solution.py:254
  35.8 22.4 %all_to_all.16 = f32[12,24,128]{2,1,0:T(8,128)S(1)} all-to-all(f32[12,24,128]{2,1,0:T(8,128)S(1)} %broadcast_in_dim.24), channel_id=1, replica_groups=mesh['z'=12,'xh'=2,'core'=2,'xl'=2,'y'=8] {'z'}, dimensions={0} | all-to-all | bytes 294912 | tf_op jit(solution)/shard_map/all_to_all | solution.py:248
  58.2 12.5 %all_to_all.17.pieces_ref = f32[4,24,128]{2,1,0:T(8,128)S(1)} all-to-all(f32[4,24,128]{2,1,0:T(8,128)S(1)} %broadcast_in_dim.25), channel_id=1, replica_groups=mesh['z'=12,'xh'=2,'core'=2,'xl'=2,'y'=8] {'xh','core'}, dimensions={0} | all-to-all | bytes 98304 | tf_op jit(solution)/shard_map/all_to_all | solution.py:248
  70.8 0.7 own_blocks.1
  (4 shorter events, 0.1 us)
Async XLA Ops:
  5.4 14.0 %collective-permute-start = (f32[32,24,128]{2,1,0:T(8,128)}, f32[32,24,128]{2,1,0:T(8,128)S(1)}, u32[]{:S(2)}, u32[]{:S(2)}) collective-permute-start(f32[32,24,128]{2,1,0:T(8,128)} %get-tuple-element.5), channel_id=1, source_target_pairs={{0,16},{16,0},{1,17},{17,1},{2,18},{18,2},{3,19},{19,3},{4,20},{20... | collective-permute-start | bytes 1179656 | tf_op jit(solution)/shard_map/ppermute | solution.py:253

commit v4 on v3

--- a/solution.py
+++ b/solution.py
@@ -179,9 +179,10 @@
 
 def local_sums(lengths, ids, masked, table, gain, resid, normed):
     width = table.shape[1]
+    operands = (lengths, ids[None], masked[None], table, gain[None], resid, normed)
     vmem = pl.BlockSpec(memory_space=pltpu.VMEM)
     hbm = pl.BlockSpec(memory_space=pltpu.HBM)
-    out = jax.ShapeDtypeStruct((2 * OWNERS, PIECE, LANES), jnp.float32)
+    out = pltpu.VMEM((2 * OWNERS, PIECE, LANES), jnp.float32)
     return pl.pallas_call(
         sums_kernel,
         out_shape=(out, out),
@@ -201,9 +202,9 @@
             pltpu.SemaphoreType.DMA((width // COPY_STEP,)),
             pltpu.SemaphoreType.DMA((width // COPY_STEP,)),
         ],
-        compiler_params=pltpu.CompilerParams(vmem_limit_bytes=60 * 1024 * 1024),
+        compiler_params=pltpu.CompilerParams(vmem_limit_bytes=32 * 1024 * 1024),
         name="local_sums",
-    )(lengths, ids[None], masked[None], table, gain[None], resid, normed)
+    )(*(pltpu.with_memory_space_constraint(operand, pltpu.HBM) for operand in operands))
 
 
 def own_kernel(pieces_ref, layer_ref, embed_ref):

time: 71.8 us -> 69.6 us (0.969)
  other arithmetic: 1.09 us -> 0.1 us
  Pallas kernels: 5.5 us -> 4.63 us
    add x1, other arithmetic: 1.04 us -> 0.04 us  [on_device(): pair = kept + lax.ppermute(given, 'core', [(0, 1), (1, 0)])]
    pallas_call x1, Pallas kernels: 4.8 us -> 3.93 us  [local_sums(): pl.pallas_call(sums_kernel, out_shape=(out, out), in_specs=[hbm] * 7, out...]
where the time goes in v4:
time: 69.6 us; the launch traced here: 69.4 us
  blocking collectives  50.2 us (72%)
  starting transfers between devices  12.4 us (18%)
  Pallas kernels  4.63 us (7%)
  waiting for transfers between devices  1.33 us (2%)
    all_to_all x2, blocking collectives, to_all(): return lax.all_to_all(sent, axes, 0, 0, tiled=True)  34.9 us
    all_to_all x1, blocking collectives, on_device(): lax.all_to_all(pair, ('xh', 'xl', 'y'), 0, 0, tiled=True)  15.3 us
    ppermute x1, starting transfers between devices, on_device(): pair = kept + lax.ppermute(given, 'core', [(0, 1), (1, 0)])  12.4 us
    pallas_call x1, Pallas kernels, local_sums(): pl.pallas_call(sums_kernel, out_shape=(out, out), in_specs=[hbm] * 7, out...  3.93 us
  transfers between devices with their start and end apart: 1, of which 1 were waited for; matrix products, arithmetic and copies ran while one was open for 0% of the time, Pallas kernels for 0%

profile of v4, /device:TPU:1, one launch (start us, length us, event | category | flops | bytes accessed | tf_op | source)
XLA Modules:
  0.0 69.4 jit_solution(10525781670155370425)
XLA Ops:
  0.6 3.9 %local_sums.1 = (f32[32,24,128]{2,1,0:T(8,128)S(1)}, f32[32,24,128]{2,1,0:T(8,128)S(1)}) custom-call(s32[1,2]{1,0:T(1,128)} %lengths_hbm.1, s32[1,128]{1,0:T(1,128)} %bitcast.4, s32[1,128]{1,0:T(1,128)} %bitcast.5, bf16[33,5120]{1,0:T(8,128)(2,1)} %table_hbm.1, f32[1,5120]{1,0:T(1,128)} %bitcast.3, bf16[128,5120]{1,0:T(8,128)(2,1)} %resid_hbm.1, ...), custom_call_target="tpu_custom_call" | custom-call | tf_op jit(solution)/shard_map/local_sums/pallas_call | solution.py:186
  4.6 12.4 %collective-permute-start = (f32[32,24,128]{2,1,0:T(8,128)S(1)}, f32[32,24,128]{2,1,0:T(8,128)S(1)}, u32[]{:S(2)}, u32[]{:S(2)}) collective-permute-start(f32[32,24,128]{2,1,0:T(8,128)S(1)} %get-tuple-element.5), channel_id=1, source_target_pairs={{0,16},{16,0},{1,17},{17,1},{2,18},{18,2},{3,19},{19,3},{4,20},{20... | collective-permute-start | bytes 1179656 | tf_op jit(solution)/shard_map/ppermute | solution.py:254
  17.0 1.3 %collective-permute-done = f32[32,24,128]{2,1,0:T(8,128)S(1)} collective-permute-done((f32[32,24,128]{2,1,0:T(8,128)S(1)}, f32[32,24,128]{2,1,0:T(8,128)S(1)}, u32[]{:S(2)}, u32[]{:S(2)}) %collective-permute-start) | collective-permute-done | bytes 393248 | tf_op jit(solution)/shard_map/ppermute | solution.py:254
  18.4 15.3 %all_to_all.15 = f32[32,24,128]{2,1,0:T(8,128)S(1)} all-to-all(f32[32,24,128]{2,1,0:T(8,128)S(1)} %add.3), channel_id=1, replica_groups=mesh['z'=12,'xh'=2,'core'=2,'xl'=2,'y'=8] {'xh','xl','y'}, dimensions={0} | all-to-all | bytes 786432 | tf_op jit(solution)/shard_map/all_to_all | solution.py:255
  33.7 22.4 %all_to_all.16 = f32[12,24,128]{2,1,0:T(8,128)S(1)} all-to-all(f32[12,24,128]{2,1,0:T(8,128)S(1)} %broadcast_in_dim.24), channel_id=1, replica_groups=mesh['z'=12,'xh'=2,'core'=2,'xl'=2,'y'=8] {'z'}, dimensions={0} | all-to-all | bytes 294912 | tf_op jit(solution)/shard_map/all_to_all | solution.py:249
  56.1 12.5 %all_to_all.17.pieces_ref = f32[4,24,128]{2,1,0:T(8,128)S(1)} all-to-all(f32[4,24,128]{2,1,0:T(8,128)S(1)} %broadcast_in_dim.25), channel_id=1, replica_groups=mesh['z'=12,'xh'=2,'core'=2,'xl'=2,'y'=8] {'xh','core'}, dimensions={0} | all-to-all | bytes 98304 | tf_op jit(solution)/shard_map/all_to_all | solution.py:249
  68.7 0.7 %own_blocks.1 = (f32[960]{0:T(1024)}, f32[10560]{0:T(1024)}) custom-call(f32[4,24,128]{2,1,0:T(8,128)S(1)} %all_to_all.17.pieces_ref), custom_call_target="tpu_custom_call" | custom-call | tf_op jit(solution)/shard_map/own_blocks/pallas_call | solution.py:234
  (5 shorter events, 0.1 us)
Async XLA Ops:
  4.6 13.8 %collective-permute-start = (f32[32,24,128]{2,1,0:T(8,128)S(1)}, f32[32,24,128]{2,1,0:T(8,128)S(1)}, u32[]{:S(2)}, u32[]{:S(2)}) collective-permute-start(f32[32,24,128]{2,1,0:T(8,128)S(1)} %get-tuple-element.5), channel_id=1, source_target_pairs={{0,16},{16,0},{1,17},{17,1},{2,18},{18,2},{3,19},{19,3},{4,20},{20... | collective-permute-start | bytes 1179656 | tf_op jit(solution)/shard_map/ppermute | solution.py:254

commit v5 on v4

--- a/solution.py
+++ b/solution.py
@@ -11,7 +11,7 @@
 EPS = 1e-05
 SHRINK = 2.0**-8
 WIDTH_STEP = 512
-COPY_STEP = 1024
+COPY_STEP = 2560
 VOCAB_USED = 32
 OWNERS = 16
 QUARTERS = 4
@@ -251,10 +251,11 @@
 
 def on_device(lengths, ids, masked, table, gain, resid, normed):
     given, kept = local_sums(lengths, ids, masked, table, gain, resid, normed)
-    pair = kept + lax.ppermute(given, "core", [(0, 1), (1, 0)])
+    both = lax.all_gather(given, "core")
+    pair = kept + lax.dynamic_index_in_dim(both, 1 - lax.axis_index("core"), 0, False)
     piece = jnp.sum(lax.all_to_all(pair, ("xh", "xl", "y"), 0, 0, tiled=True), axis=0)
     piece = jnp.sum(to_all(piece, "z", 12), axis=0)
-    pieces = to_all(piece, ("xh", "core"), QUARTERS)
+    pieces = lax.all_gather(piece, ("xh", "core"))
     return own_blocks(
         pieces, 3 * table.shape[1] // OWNERS, table.shape[0] * table.shape[1] // OWNERS
     )

time: 69.6 us -> 66.6 us (0.957)
  starting transfers between devices: 12.4 us -> 0 us
  blocking collectives: 50.2 us -> 61.2 us
  waiting for transfers between devices: 1.33 us -> 0 us
  Pallas kernels: 4.63 us -> 3.85 us
    all_gather x0 -> x2, blocking collectives: none -> 23.5 us  [the longest x1 12.5 us: on_device(): both = lax.all_gather(given, 'core')]
    all_to_all x2 -> x1, blocking collectives: 34.9 us -> 22.4 us  [to_all(): return lax.all_to_all(sent, axes, 0, 0, tiled=True)]
    ppermute x1 -> x0, starting transfers between devices: 12.4 us -> none  [on_device(): pair = kept + lax.ppermute(given, 'core', [(0, 1), (1, 0)])]
    ppermute x1 -> x0, waiting for transfers between devices: 1.33 us -> none  [on_device(): pair = kept + lax.ppermute(given, 'core', [(0, 1), (1, 0)])]
    pallas_call x1, Pallas kernels: 3.93 us -> 3.15 us  [local_sums(): pl.pallas_call(sums_kernel, out_shape=(out, out), in_specs=[hbm] * 7, out...]
  transfers between devices with their start and end apart: 1 -> 0, of which waited for: 1 -> 0; matrix products, arithmetic and copies ran while one was open for 0% -> 0% of each run, Pallas kernels for 0% -> 0%
where the time goes in v5:
time: 66.6 us; the launch traced here: 65.8 us
  blocking collectives  61.2 us (92%)
  Pallas kernels  3.85 us (6%)
    all_to_all x1, blocking collectives, to_all(): return lax.all_to_all(sent, axes, 0, 0, tiled=True)  22.4 us
    all_to_all x1, blocking collectives, on_device(): lax.all_to_all(pair, ('xh', 'xl', 'y'), 0, 0, tiled=True)  15.3 us
    all_gather x1, blocking collectives, on_device(): both = lax.all_gather(given, 'core')  12.5 us
    all_gather x1, blocking collectives, on_device(): pieces = lax.all_gather(piece, ('xh', 'core'))  11 us
    pallas_call x1, Pallas kernels, local_sums(): pl.pallas_call(sums_kernel, out_shape=(out, out), in_specs=[hbm] * 7, out...  3.15 us

profile of v5, /device:TPU:1, one launch (start us, length us, event | category | flops | bytes accessed | tf_op | source)
XLA Modules:
  0.0 65.8 jit_solution(7764808571509804621)
XLA Ops:
  0.6 3.2 %local_sums.1 = (f32[32,24,128]{2,1,0:T(8,128)S(1)}, f32[32,24,128]{2,1,0:T(8,128)S(1)}) custom-call(s32[1,2]{1,0:T(1,128)} %lengths_hbm.1, s32[1,128]{1,0:T(1,128)} %bitcast.10, s32[1,128]{1,0:T(1,128)} %bitcast.11, bf16[33,5120]{1,0:T(8,128)(2,1)} %table_hbm.1, f32[1,5120]{1,0:T(1,128)} %bitcast.9, bf16[128,5120]{1,0:T(8,128)(2,1)} %resid_hbm.1, ...), custom_call_target="tpu_custom_call" | custom-call | tf_op jit(solution)/shard_map/local_sums/pallas_call | solution.py:186
  3.8 12.5 %all-gather = f32[64,24,128]{2,1,0:T(8,128)S(1)} all-gather(f32[32,24,128]{2,1,0:T(8,128)S(1)} %get-tuple-element.5), channel_id=2, replica_groups=mesh['z'=12,'xh'=2,'core'=2,'xl'=2,'y'=8] {'core'}, dimensions={0}, use_global_device_ids=true | all-gather | bytes 1179648 | tf_op jit(solution)/shard_map/all_gather | solution.py:254
  16.4 15.3 %all_to_all.10 = f32[32,24,128]{2,1,0:T(8,128)S(1)} all-to-all(f32[32,24,128]{2,1,0:T(8,128)S(1)} %bitcast_add_fusion), channel_id=1, replica_groups=mesh['z'=12,'xh'=2,'core'=2,'xl'=2,'y'=8] {'xh','xl','y'}, dimensions={0} | all-to-all | bytes 786432 | tf_op jit(solution)/shard_map/all_to_all | solution.py:256
  31.7 22.4 %all_to_all.11 = f32[12,24,128]{2,1,0:T(8,128)S(1)} all-to-all(f32[12,24,128]{2,1,0:T(8,128)S(1)} %broadcast_in_dim.18), channel_id=1, replica_groups=mesh['z'=12,'xh'=2,'core'=2,'xl'=2,'y'=8] {'z'}, dimensions={0} | all-to-all | bytes 294912 | tf_op jit(solution)/shard_map/all_to_all | solution.py:249
  54.1 11.0 %all-gather.1 = f32[96,128]{1,0:T(8,128)S(1)} all-gather(f32[24,128]{1,0:T(8,128)S(1)} %reduce_sum.19), channel_id=3, replica_groups=mesh['z'=12,'xh'=2,'core'=2,'xl'=2,'y'=8] {'xh','core'}, dimensions={0}, use_global_device_ids=true | all-gather | bytes 61440 | tf_op jit(solution)/shard_map/all_gather | solution.py:258
  65.1 0.7 %own_blocks.1 = (f32[960]{0:T(1024)}, f32[10560]{0:T(1024)}) custom-call(f32[4,24,128]{2,1,0:T(8,128)S(1)} %bitcast.7), custom_call_target="tpu_custom_call" | custom-call | tf_op jit(solution)/shard_map/own_blocks/pallas_call | solution.py:234
  (4 shorter events, 0.1 us)

commit v6 on v5

--- a/solution.py
+++ b/solution.py
@@ -11,7 +11,6 @@
 EPS = 1e-05
 SHRINK = 2.0**-8
 WIDTH_STEP = 512
-COPY_STEP = 2560
 VOCAB_USED = 32
 OWNERS = 16
 QUARTERS = 4
@@ -34,17 +33,14 @@
     return live, live * (1.0 - masked) * scale
 
 
-def split3(value):
+def split2(value):
     high = value.astype(jnp.bfloat16)
-    rest = value - high.astype(jnp.float32)
-    mid = rest.astype(jnp.bfloat16)
-    low = (rest - mid.astype(jnp.float32)).astype(jnp.bfloat16)
-    return [high, mid, low]
-
-
-def sum3(parts, at):
+    return [high, (value - high.astype(jnp.float32)).astype(jnp.bfloat16)]
+
+
+def sum2(parts, at):
     n = VOCAB_USED
-    return parts[at : at + n] + parts[at + n : at + 2 * n] + parts[at + 2 * n : at + 3 * n]
+    return parts[at : at + n] + parts[at + n : at + 2 * n]
 
 
 def lane_fold(value):
@@ -58,7 +54,7 @@
     lengths_hbm, ids_hbm, masked_hbm, table_hbm, gain_hbm, resid_hbm, normed_hbm,
     given_ref, kept_ref,
     lengths_ref, ids_ref, masked_ref, table_ref, gain_ref, resid_ref, normed_ref,
-    total_ref, flat_ref, small_sem, resid_sem, normed_sem,
+    center_ref, slope_gain_ref, total_ref, resid_row_ref, flat_ref, small_sem, resid_sem, normed_sem,
 ):
     small_copies = [
         pltpu.make_async_copy(source, target, small_sem.at[i])
@@ -72,19 +68,9 @@
             )
         )
     ]
-    large_copies = []
-    for i in range(table_ref.shape[1] // COPY_STEP):
-        columns = pl.ds(i * COPY_STEP, COPY_STEP)
-        large_copies.append(
-            [
-                pltpu.make_async_copy(source.at[:, columns], target.at[:, columns], sem.at[i])
-                for source, target, sem in (
-                    (resid_hbm, resid_ref, resid_sem),
-                    (normed_hbm, normed_ref, normed_sem),
-                )
-            ]
-        )
-    for copy in small_copies + sum(large_copies, []):
+    resid_copy = pltpu.make_async_copy(resid_hbm, resid_ref, resid_sem)
+    normed_copy = pltpu.make_async_copy(normed_hbm, normed_ref, normed_sem)
+    for copy in [*small_copies, resid_copy, normed_copy]:
         copy.start()
     for copy in small_copies:
         copy.wait()
@@ -99,6 +85,11 @@
     variance = jnp.minimum(spread * SHRINK**-2, 1e38)
     unit = lax.rsqrt(variance + EPS)
     unscaled = (variance + EPS) * unit
+    for at in range(0, width, WIDTH_STEP):
+        columns = slice(at, at + WIDTH_STEP)
+        centered = (table_ref[0:n, columns].astype(jnp.float32) * SHRINK - mean) * SHRINK**-1
+        center_ref[:, columns] = centered
+        slope_gain_ref[:, columns] = centered * unit * gain_ref[:, columns]
 
     hit = ids_ref[...] == lax.broadcasted_iota(jnp.int32, (n, slots), 0)
     weighted = jnp.where(hit, weight, 0.0)
@@ -106,36 +97,36 @@
     ratio = through * unscaled
     row = lax.broadcasted_iota(jnp.int32, (16, slots), 0)
     alive = jnp.where(row == 0, live, 0.0).astype(jnp.bfloat16)
-    left_resid = jnp.concatenate([*split3(weighted), alive], axis=0)
+    left_resid = jnp.concatenate([*split2(weighted), alive], axis=0)
     left_normed = jnp.concatenate(
-        [*split3(through), *split3(through * ratio * ratio), alive], axis=0
+        [*split2(through), *split2(through * ratio * ratio), alive], axis=0
     )
 
     mean_sum = jnp.zeros((n, LANES), jnp.float32)
     slope_sum = jnp.zeros((n, LANES), jnp.float32)
+    resid_copy.wait()
     for at in range(0, width, WIDTH_STEP):
-        if at % COPY_STEP == 0:
-            for copy in large_copies[at // COPY_STEP]:
-                copy.wait()
         columns = slice(at, at + WIDTH_STEP)
         from_resid = jnp.dot(left_resid, resid_ref[:, columns], preferred_element_type=jnp.float32)
+        total_ref[:, columns] = sum2(from_resid, 0)
+        resid_row_ref[:, columns] = from_resid[2 * n : 2 * n + 1]
+    normed_copy.wait()
+    for at in range(0, width, WIDTH_STEP):
+        columns = slice(at, at + WIDTH_STEP)
         from_normed = jnp.dot(
             left_normed, normed_ref[:, columns], preferred_element_type=jnp.float32
         )
-        gain = gain_ref[:, columns]
-        centered = table_ref[0:n, columns].astype(jnp.float32) * SHRINK - mean
-        centered = centered * SHRINK**-1
-        passed = sum3(from_normed, 0)
-        gained = passed * gain
+        passed = sum2(from_normed, 0)
+        gained = passed * gain_ref[:, columns]
         mean_sum += lane_fold(gained)
-        slope_sum += lane_fold(centered * unit * gain * sum3(from_normed, 3 * n))
-        total_ref[:, columns] = sum3(from_resid, 0) + gained
-        gain_grad = jnp.sum(centered * passed, axis=0, keepdims=True)
+        slope_sum += lane_fold(slope_gain_ref[:, columns] * sum2(from_normed, 2 * n))
+        total_ref[:, columns] += gained
+        gain_grad = jnp.sum(center_ref[:, columns] * passed, axis=0, keepdims=True)
         row = lax.broadcasted_iota(jnp.int32, (SUBLANES, WIDTH_STEP), 0)
         layer = jnp.where(
             row == 1,
-            from_resid[3 * n : 3 * n + 1],
-            jnp.where(row == 2, gain_grad, jnp.where(row == 3, from_normed[6 * n : 6 * n + 1], 0.0)),
+            resid_row_ref[:, columns],
+            jnp.where(row == 2, gain_grad, jnp.where(row == 3, from_normed[4 * n : 4 * n + 1], 0.0)),
         )
         for k in range(WIDTH_STEP // LANES):
             at_row = n * blocks + at // LANES + k
@@ -146,8 +137,7 @@
     slope = jnp.sum(slope_sum, axis=1, keepdims=True) / width * unit
     for k in range(blocks):
         columns = slice(k * LANES, (k + 1) * LANES)
-        centered = table_ref[0:n, columns].astype(jnp.float32) * SHRINK - mean
-        result = total_ref[:, columns] - mean_sum - centered * SHRINK**-1 * slope
+        result = total_ref[:, columns] - mean_sum - center_ref[:, columns] * slope
         for tile in range(n // SUBLANES):
             rows = slice(tile * SUBLANES, (tile + 1) * SUBLANES)
             flat_ref[pl.ds(tile * SUBLANES * blocks + k, SUBLANES, stride=blocks), :] = result[rows]
@@ -197,10 +187,13 @@
             pltpu.VMEM(resid.shape, resid.dtype),
             pltpu.VMEM(normed.shape, normed.dtype),
             pltpu.VMEM((VOCAB_USED, width), jnp.float32),
+            pltpu.VMEM((VOCAB_USED, width), jnp.float32),
+            pltpu.VMEM((VOCAB_USED, width), jnp.float32),
+            pltpu.VMEM((1, width), jnp.float32),
             pltpu.VMEM(((VOCAB_USED + SUBLANES) * width // LANES, LANES), jnp.float32),
             pltpu.SemaphoreType.DMA((5,)),
-            pltpu.SemaphoreType.DMA((width // COPY_STEP,)),
-            pltpu.SemaphoreType.DMA((width // COPY_STEP,)),
+            pltpu.SemaphoreType.DMA,
+            pltpu.SemaphoreType.DMA,
         ],
         compiler_params=pltpu.CompilerParams(vmem_limit_bytes=32 * 1024 * 1024),
         name="local_sums",

time: 66.6 us -> 66.2 us (level)
  no operation moved by 1% of the time
where the time goes in v6:
time: 66.2 us; the launch traced here: 65.4 us
  blocking collectives  61.2 us (92%)
  Pallas kernels  3.45 us (5%)
    all_to_all x1, blocking collectives, to_all(): return lax.all_to_all(sent, axes, 0, 0, tiled=True)  22.4 us
    all_to_all x1, blocking collectives, on_device(): lax.all_to_all(pair, ('xh', 'xl', 'y'), 0, 0, tiled=True)  15.3 us
    all_gather x1, blocking collectives, on_device(): both = lax.all_gather(given, 'core')  12.5 us
    all_gather x1, blocking collectives, on_device(): pieces = lax.all_gather(piece, ('xh', 'core'))  11 us
    pallas_call x1, Pallas kernels, local_sums(): pl.pallas_call(sums_kernel, out_shape=(out, out), in_specs=[hbm] * 7, out...  2.75 us

profile of v6, /device:TPU:1, one launch (start us, length us, event | category | flops | bytes accessed | tf_op | source)
XLA Modules:
  0.0 65.4 jit_solution(415912818110578178)
XLA Ops:
  0.6 2.8 %local_sums.1 = (f32[32,24,128]{2,1,0:T(8,128)S(1)}, f32[32,24,128]{2,1,0:T(8,128)S(1)}) custom-call(s32[1,2]{1,0:T(1,128)} %lengths_hbm.1, s32[1,128]{1,0:T(1,128)} %bitcast.10, s32[1,128]{1,0:T(1,128)} %bitcast.11, bf16[33,5120]{1,0:T(8,128)(2,1)} %table_hbm.1, f32[1,5120]{1,0:T(1,128)} %bitcast.9, bf16[128,5120]{1,0:T(8,128)(2,1)} %resid_hbm.1, ...), custom_call_target="tpu_custom_call" | custom-call | tf_op jit(solution)/shard_map/local_sums/pallas_call | solution.py:176
  3.4 12.5 %all-gather = f32[64,24,128]{2,1,0:T(8,128)S(1)} all-gather(f32[32,24,128]{2,1,0:T(8,128)S(1)} %get-tuple-element.5), channel_id=2, replica_groups=mesh['z'=12,'xh'=2,'core'=2,'xl'=2,'y'=8] {'core'}, dimensions={0}, use_global_device_ids=true | all-gather | bytes 1179648 | tf_op jit(solution)/shard_map/all_gather | solution.py:247
  16.0 15.3 %all_to_all.10 = f32[32,24,128]{2,1,0:T(8,128)S(1)} all-to-all(f32[32,24,128]{2,1,0:T(8,128)S(1)} %bitcast_add_fusion), channel_id=1, replica_groups=mesh['z'=12,'xh'=2,'core'=2,'xl'=2,'y'=8] {'xh','xl','y'}, dimensions={0} | all-to-all | bytes 786432 | tf_op jit(solution)/shard_map/all_to_all | solution.py:249
  31.3 22.4 %all_to_all.11 = f32[12,24,128]{2,1,0:T(8,128)S(1)} all-to-all(f32[12,24,128]{2,1,0:T(8,128)S(1)} %broadcast_in_dim.18), channel_id=1, replica_groups=mesh['z'=12,'xh'=2,'core'=2,'xl'=2,'y'=8] {'z'}, dimensions={0} | all-to-all | bytes 294912 | tf_op jit(solution)/shard_map/all_to_all | solution.py:242
  53.7 11.0 %all-gather.1 = f32[96,128]{1,0:T(8,128)S(1)} all-gather(f32[24,128]{1,0:T(8,128)S(1)} %reduce_sum.19), channel_id=3, replica_groups=mesh['z'=12,'xh'=2,'core'=2,'xl'=2,'y'=8] {'xh','core'}, dimensions={0}, use_global_device_ids=true | all-gather | bytes 61440 | tf_op jit(solution)/shard_map/all_gather | solution.py:251
  64.7 0.7 %own_blocks.1 = (f32[960]{0:T(1024)}, f32[10560]{0:T(1024)}) custom-call(f32[4,24,128]{2,1,0:T(8,128)S(1)} %bitcast.7), custom_call_target="tpu_custom_call" | custom-call | tf_op jit(solution)/shard_map/own_blocks/pallas_call | solution.py:227
  (4 shorter events, 0.1 us)

commit v7 on v6

--- a/solution.py
+++ b/solution.py
@@ -14,6 +14,8 @@
 VOCAB_USED = 32
 OWNERS = 16
 QUARTERS = 4
+PLANE = [x * 8 + y for x in (3, 2, 1, 0) for y in (5, 6, 4, 7, 3, 2, 1, 0)]
+PLANES = [8, 7, 9, 6, 10, 5, 11, 4, 3, 2, 1, 0]
 PIECE = 24
 HOLDERS = ("z", "xh", "core", "xl", "y")
 
@@ -154,7 +156,7 @@
                     start = layer_row + owner * 15 // 2
                 else:
                     start = owner * 165 // 2 + (tile - 1) * SUBLANES
-                out_ref[quarter // 2 * OWNERS + owner, pl.ds(inner * SUBLANES, SUBLANES), :] = (
+                out_ref[PLANE.index(quarter // 2 * OWNERS + owner), pl.ds(inner * SUBLANES, SUBLANES), :] = (
                     flat_ref[pl.ds(start, SUBLANES), :]
                 )
 
@@ -237,17 +239,17 @@
     )(pieces)
 
 
-def to_all(block, axes, count):
-    sent = jnp.broadcast_to(block[None], (count, *block.shape))
-    return lax.all_to_all(sent, axes, 0, 0, tiled=True)
+def to_all(block, axes, order):
+    sent = jnp.broadcast_to(block[None], (len(order), *block.shape))
+    return lax.all_to_all(sent, axes, 0, 0, axis_index_groups=[order], tiled=True)
 
 
 def on_device(lengths, ids, masked, table, gain, resid, normed):
     given, kept = local_sums(lengths, ids, masked, table, gain, resid, normed)
     both = lax.all_gather(given, "core")
     pair = kept + lax.dynamic_index_in_dim(both, 1 - lax.axis_index("core"), 0, False)
-    piece = jnp.sum(lax.all_to_all(pair, ("xh", "xl", "y"), 0, 0, tiled=True), axis=0)
-    piece = jnp.sum(to_all(piece, "z", 12), axis=0)
+    piece = jnp.sum(lax.all_to_all(pair, ("xh", "xl", "y"), 0, 0, axis_index_groups=[PLANE], tiled=True), axis=0)
+    piece = jnp.sum(to_all(piece, "z", PLANES), axis=0)
     pieces = lax.all_gather(piece, ("xh", "core"))
     return own_blocks(
         pieces, 3 * table.shape[1] // OWNERS, table.shape[0] * table.shape[1] // OWNERS

time: 66.2 us -> 61 us (0.921)
  blocking collectives: 61.2 us -> 56.5 us
    all_gather x1, blocking collectives: 11 us -> 8.52 us  [on_device(): pieces = lax.all_gather(piece, ('xh', 'core'))]
    all_to_all x2, blocking collectives: 37.7 us -> 35.5 us  [the longest x1 18.6 us: on_device(): lax.all_to_all(pair, ('xh', 'xl', 'y'), 0, 0, axis_index_groups=[PLANE],...]
where the time goes in v7:
time: 61 us; the launch traced here: 60.7 us
  blocking collectives  56.5 us (93%)
  Pallas kernels  3.45 us (6%)
  between operations  0.66 us (1%)
    all_to_all x1, blocking collectives, on_device(): lax.all_to_all(pair, ('xh', 'xl', 'y'), 0, 0, axis_index_groups=[PLANE],...  18.6 us
    all_to_all x1, blocking collectives, to_all(): lax.all_to_all(sent, axes, 0, 0, axis_index_groups=[order], tiled=True)  16.9 us
    all_gather x1, blocking collectives, on_device(): both = lax.all_gather(given, 'core')  12.5 us
    all_gather x1, blocking collectives, on_device(): pieces = lax.all_gather(piece, ('xh', 'core'))  8.52 us
    pallas_call x1, Pallas kernels, local_sums(): pl.pallas_call(sums_kernel, out_shape=(out, out), in_specs=[hbm] * 7, out...  2.75 us

profile of v7, /device:TPU:1, one launch (start us, length us, event | category | flops | bytes accessed | tf_op | source)
XLA Modules:
  0.0 60.7 jit_solution(3995659365090053142)
XLA Ops:
  0.6 2.8 %local_sums.1 = (f32[32,24,128]{2,1,0:T(8,128)S(1)}, f32[32,24,128]{2,1,0:T(8,128)S(1)}) custom-call(s32[1,2]{1,0:T(1,128)} %lengths_hbm.1, s32[1,128]{1,0:T(1,128)} %bitcast.10, s32[1,128]{1,0:T(1,128)} %bitcast.11, bf16[33,5120]{1,0:T(8,128)(2,1)} %table_hbm.1, f32[1,5120]{1,0:T(1,128)} %bitcast.9, bf16[128,5120]{1,0:T(8,128)(2,1)} %resid_hbm.1, ...), custom_call_target="tpu_custom_call" | custom-call | tf_op jit(solution)/shard_map/local_sums/pallas_call | solution.py:178
  3.4 12.5 %all-gather = f32[64,24,128]{2,1,0:T(8,128)S(1)} all-gather(f32[32,24,128]{2,1,0:T(8,128)S(1)} %get-tuple-element.5), channel_id=2, replica_groups=mesh['z'=12,'xh'=2,'core'=2,'xl'=2,'y'=8] {'core'}, dimensions={0}, use_global_device_ids=true | all-gather | bytes 1179648 | tf_op jit(solution)/shard_map/all_gather | solution.py:249
  16.0 18.6 %all_to_all.10 = f32[32,24,128]{2,1,0:T(8,128)S(1)} all-to-all(f32[32,24,128]{2,1,0:T(8,128)S(1)} %bitcast_add_fusion), channel_id=1, replica_groups={{45,46,44,47,43,42,41,40,37,38,36,39,35,34,33,32,13,14,12,15,11,10,9,8,..., dimensions={0} | all-to-all | bytes 786432 | tf_op jit(solution)/shard_map/all_to_all | solution.py:251
  34.6 16.9 %all_to_all.11 = f32[12,24,128]{2,1,0:T(8,128)S(1)} all-to-all(f32[12,24,128]{2,1,0:T(8,128)S(1)} %broadcast_in_dim.18), channel_id=1, replica_groups={{512,448,576,384,640,320,704,256,192,128,64,0},{513,449,577,385,641,321..., dimensions={0} | all-to-all | bytes 294912 | tf_op jit(solution)/shard_map/all_to_all | solution.py:244
  51.5 8.5 %all-gather.1 = f32[96,128]{1,0:T(8,128)S(1)} all-gather(f32[24,128]{1,0:T(8,128)S(1)} %reduce_sum.19), channel_id=3, replica_groups=mesh['z'=12,'xh'=2,'core'=2,'xl'=2,'y'=8] {'xh','core'}, dimensions={0}, use_global_device_ids=true | all-gather | bytes 61440 | tf_op jit(solution)/shard_map/all_gather | solution.py:253
  60.0 0.7 %own_blocks.1 = (f32[960]{0:T(1024)}, f32[10560]{0:T(1024)}) custom-call(f32[4,24,128]{2,1,0:T(8,128)S(1)} %bitcast.7), custom_call_target="tpu_custom_call" | custom-call | tf_op jit(solution)/shard_map/own_blocks/pallas_call | solution.py:229
  (4 shorter events, 0.1 us)

commit v8 on v7

--- a/solution.py
+++ b/solution.py
@@ -14,7 +14,7 @@
 VOCAB_USED = 32
 OWNERS = 16
 QUARTERS = 4
-PLANE = [x * 8 + y for x in (3, 2, 1, 0) for y in (5, 6, 4, 7, 3, 2, 1, 0)]
+PLANE = [x * 8 + y for y in (5, 6, 4, 7, 3, 2, 1, 0) for x in (3, 2, 1, 0)]
 PLANES = [8, 7, 9, 6, 10, 5, 11, 4, 3, 2, 1, 0]
 PIECE = 24
 HOLDERS = ("z", "xh", "core", "xl", "y")

time: 61 us -> 59.5 us (0.975)
  blocking collectives: 56.5 us -> 55.1 us
    all_to_all x1, blocking collectives: 18.6 us -> 17.2 us  [on_device(): lax.all_to_all(pair, ('xh', 'xl', 'y'), 0, 0, axis_index_groups=[PLANE],...]
    all_gather x1, blocking collectives: 8.52 us -> 9.19 us  [on_device(): pieces = lax.all_gather(piece, ('xh', 'core'))]
    all_to_all x1, blocking collectives: 16.9 us -> 16.2 us  [to_all(): lax.all_to_all(sent, axes, 0, 0, axis_index_groups=[order], tiled=True)]
where the time goes in v8:
time: 59.5 us; the launch traced here: 59.3 us
  blocking collectives  55.1 us (93%)
  Pallas kernels  3.45 us (6%)
  between operations  0.66 us (1%)
    all_to_all x1, blocking collectives, on_device(): lax.all_to_all(pair, ('xh', 'xl', 'y'), 0, 0, axis_index_groups=[PLANE],...  17.2 us
    all_to_all x1, blocking collectives, to_all(): lax.all_to_all(sent, axes, 0, 0, axis_index_groups=[order], tiled=True)  16.2 us
    all_gather x1, blocking collectives, on_device(): both = lax.all_gather(given, 'core')  12.5 us
    all_gather x1, blocking collectives, on_device(): pieces = lax.all_gather(piece, ('xh', 'core'))  9.19 us
    pallas_call x1, Pallas kernels, local_sums(): pl.pallas_call(sums_kernel, out_shape=(out, out), in_specs=[hbm] * 7, out...  2.75 us

profile of v8, /device:TPU:1, one launch (start us, length us, event | category | flops | bytes accessed | tf_op | source)
XLA Modules:
  0.0 59.3 jit_solution(11856554586249644144)
XLA Ops:
  0.6 2.8 %local_sums.1 = (f32[32,24,128]{2,1,0:T(8,128)S(1)}, f32[32,24,128]{2,1,0:T(8,128)S(1)}) custom-call(s32[1,2]{1,0:T(1,128)} %lengths_hbm.1, s32[1,128]{1,0:T(1,128)} %bitcast.10, s32[1,128]{1,0:T(1,128)} %bitcast.11, bf16[33,5120]{1,0:T(8,128)(2,1)} %table_hbm.1, f32[1,5120]{1,0:T(1,128)} %bitcast.9, bf16[128,5120]{1,0:T(8,128)(2,1)} %resid_hbm.1, ...), custom_call_target="tpu_custom_call" | custom-call | tf_op jit(solution)/shard_map/local_sums/pallas_call | solution.py:178
  3.4 12.5 %all-gather = f32[64,24,128]{2,1,0:T(8,128)S(1)} all-gather(f32[32,24,128]{2,1,0:T(8,128)S(1)} %get-tuple-element.5), channel_id=2, replica_groups=mesh['z'=12,'xh'=2,'core'=2,'xl'=2,'y'=8] {'core'}, dimensions={0}, use_global_device_ids=true | all-gather | bytes 1179648 | tf_op jit(solution)/shard_map/all_gather | solution.py:249
  16.0 17.2 %all_to_all.10 = f32[32,24,128]{2,1,0:T(8,128)S(1)} all-to-all(f32[32,24,128]{2,1,0:T(8,128)S(1)} %bitcast_add_fusion), channel_id=1, replica_groups={{45,37,13,5,46,38,14,6,44,36,12,4,47,39,15,7,43,35,11,3,42,34,10,2,41,3..., dimensions={0} | all-to-all | bytes 786432 | tf_op jit(solution)/shard_map/all_to_all | solution.py:251
  33.2 16.2 %all_to_all.11 = f32[12,24,128]{2,1,0:T(8,128)S(1)} all-to-all(f32[12,24,128]{2,1,0:T(8,128)S(1)} %broadcast_in_dim.18), channel_id=1, replica_groups={{512,448,576,384,640,320,704,256,192,128,64,0},{513,449,577,385,641,321..., dimensions={0} | all-to-all | bytes 294912 | tf_op jit(solution)/shard_map/all_to_all | solution.py:244
  49.4 9.2 %all-gather.1 = f32[96,128]{1,0:T(8,128)S(1)} all-gather(f32[24,128]{1,0:T(8,128)S(1)} %reduce_sum.19), channel_id=3, replica_groups=mesh['z'=12,'xh'=2,'core'=2,'xl'=2,'y'=8] {'xh','core'}, dimensions={0}, use_global_device_ids=true | all-gather | bytes 61440 | tf_op jit(solution)/shard_map/all_gather | solution.py:253
  58.6 0.7 %own_blocks.1 = (f32[960]{0:T(1024)}, f32[10560]{0:T(1024)}) custom-call(f32[4,24,128]{2,1,0:T(8,128)S(1)} %bitcast.7), custom_call_target="tpu_custom_call" | custom-call | tf_op jit(solution)/shard_map/own_blocks/pallas_call | solution.py:229
  (4 shorter events, 0.1 us)

commit v9 on v8

--- a/solution.py
+++ b/solution.py
@@ -15,7 +15,7 @@
 OWNERS = 16
 QUARTERS = 4
 PLANE = [x * 8 + y for y in (5, 6, 4, 7, 3, 2, 1, 0) for x in (3, 2, 1, 0)]
-PLANES = [8, 7, 9, 6, 10, 5, 11, 4, 3, 2, 1, 0]
+PLANES = [8, 9, 7, 10, 6, 11, 5, 4, 3, 2, 1, 0]
 PIECE = 24
 HOLDERS = ("z", "xh", "core", "xl", "y")
 

time: 59.5 us -> 59.5 us (level)
  no operation moved by 1% of the time
where the time goes in v9:
time: 59.5 us; the launch traced here: 59.3 us
  blocking collectives  55.1 us (93%)
  Pallas kernels  3.45 us (6%)
  between operations  0.66 us (1%)
    all_to_all x1, blocking collectives, on_device(): lax.all_to_all(pair, ('xh', 'xl', 'y'), 0, 0, axis_index_groups=[PLANE],...  17.2 us
    all_to_all x1, blocking collectives, to_all(): lax.all_to_all(sent, axes, 0, 0, axis_index_groups=[order], tiled=True)  16.2 us
    all_gather x1, blocking collectives, on_device(): both = lax.all_gather(given, 'core')  12.5 us
    all_gather x1, blocking collectives, on_device(): pieces = lax.all_gather(piece, ('xh', 'core'))  9.19 us
    pallas_call x1, Pallas kernels, local_sums(): pl.pallas_call(sums_kernel, out_shape=(out, out), in_specs=[hbm] * 7, out...  2.75 us

profile of v9, /device:TPU:1, one launch (start us, length us, event | category | flops | bytes accessed | tf_op | source)
XLA Modules:
  0.0 59.3 jit_solution(6509702607616533551)
XLA Ops:
  0.6 2.8 %local_sums.1 = (f32[32,24,128]{2,1,0:T(8,128)S(1)}, f32[32,24,128]{2,1,0:T(8,128)S(1)}) custom-call(s32[1,2]{1,0:T(1,128)} %lengths_hbm.1, s32[1,128]{1,0:T(1,128)} %bitcast.10, s32[1,128]{1,0:T(1,128)} %bitcast.11, bf16[33,5120]{1,0:T(8,128)(2,1)} %table_hbm.1, f32[1,5120]{1,0:T(1,128)} %bitcast.9, bf16[128,5120]{1,0:T(8,128)(2,1)} %resid_hbm.1, ...), custom_call_target="tpu_custom_call" | custom-call | tf_op jit(solution)/shard_map/local_sums/pallas_call | solution.py:178
  3.4 12.5 %all-gather = f32[64,24,128]{2,1,0:T(8,128)S(1)} all-gather(f32[32,24,128]{2,1,0:T(8,128)S(1)} %get-tuple-element.5), channel_id=2, replica_groups=mesh['z'=12,'xh'=2,'core'=2,'xl'=2,'y'=8] {'core'}, dimensions={0}, use_global_device_ids=true | all-gather | bytes 1179648 | tf_op jit(solution)/shard_map/all_gather | solution.py:249
  16.0 17.2 %all_to_all.10 = f32[32,24,128]{2,1,0:T(8,128)S(1)} all-to-all(f32[32,24,128]{2,1,0:T(8,128)S(1)} %bitcast_add_fusion), channel_id=1, replica_groups={{45,37,13,5,46,38,14,6,44,36,12,4,47,39,15,7,43,35,11,3,42,34,10,2,41,3..., dimensions={0} | all-to-all | bytes 786432 | tf_op jit(solution)/shard_map/all_to_all | solution.py:251
  33.2 16.2 %all_to_all.11 = f32[12,24,128]{2,1,0:T(8,128)S(1)} all-to-all(f32[12,24,128]{2,1,0:T(8,128)S(1)} %broadcast_in_dim.18), channel_id=1, replica_groups={{512,576,448,640,384,704,320,256,192,128,64,0},{513,577,449,641,385,705..., dimensions={0} | all-to-all | bytes 294912 | tf_op jit(solution)/shard_map/all_to_all | solution.py:244
  49.4 9.2 %all-gather.1 = f32[96,128]{1,0:T(8,128)S(1)} all-gather(f32[24,128]{1,0:T(8,128)S(1)} %reduce_sum.19), channel_id=3, replica_groups=mesh['z'=12,'xh'=2,'core'=2,'xl'=2,'y'=8] {'xh','core'}, dimensions={0}, use_global_device_ids=true | all-gather | bytes 61440 | tf_op jit(solution)/shard_map/all_gather | solution.py:253
  58.6 0.7 %own_blocks.1 = (f32[960]{0:T(1024)}, f32[10560]{0:T(1024)}) custom-call(f32[4,24,128]{2,1,0:T(8,128)S(1)} %bitcast.7), custom_call_target="tpu_custom_call" | custom-call | tf_op jit(solution)/shard_map/own_blocks/pallas_call | solution.py:229
  (4 shorter events, 0.1 us)
